TPU v7x, 32 devices: a whole 2x2x4 slice. The times are simulated.
32 devices in a mesh: dp: 8 (over z, y), head: 4 (over x, core).
Axes of the slice: x: 2, y: 2, z: 4, core: 2. Of those that a mesh axis runs over, the one named last changes fastest.
Arguments:
- block_in: bfloat16 [4096, 2304], P(('dp', 'head')), may hold values from -6 to 6
- cotangent: bfloat16 [4096, 2304], P(('dp', 'head')), may hold values from -6 to 6
- seq_ids: int32 [4096], P(('dp', 'head')), may hold values from 0 to 3, as said below
- weights: float32 [2304, 132, 256], P('dp', 'head')
- momentum: float32 [2304, 132, 256], P('dp', 'head')
- gains: float32 [2, 2304], replicated, may hold values from 0.5 to 1.5
- gain_first: float32 [2, 2304], replicated
- gain_second: float32 [2, 2304], replicated, as said below
Outputs:
- block_out: bfloat16 [4096, 2304], P(('dp', 'head'))
- grad_input: float32 [4096, 2304], P(('dp', 'head'))
- weight_grads: float32 [2304, 132, 256], P('dp', 'head')
- new_momentum: float32 [2304, 132, 256], P('dp', 'head')
- new_weights: float32 [2304, 132, 256], P('dp', 'head')
- gain_grads: float32 [2, 2304], replicated
- new_gain_first: float32 [2, 2304], replicated
- new_gain_second: float32 [2, 2304], replicated
- new_gains: float32 [2, 2304], replicated
Inputs may be any that keep to these rules, and one draw needn't show every extreme that they name: seq_ids never fall along the tokens; no sequence is longer than 4096 tokens; sequence 0 is shorter than 512 tokens; sequences 1 to 1 are the long ones, and each boundary between two of them lies between a quarter and a half of 512 tokens after a multiple of 4096; the last two sequences together are shorter than 512 tokens. `gain_second`: positive.
All inputs are finite; a program needn't handle non-finite values.
Results may differ from a plain program's by a relative error of at most 0.02.
The roundings to bfloat16 on the way count: a program that leaves them out, or rounds other values in their place, can miss the bound.
Values may be sent and summed in bfloat16 or wider, within the bound.
No kernel may reach another device: no remote copies, remote signals or barrier semaphores. Data moves between devices by JAX's collectives and lax.ppermute only.
A program may use at most 448 MiB of HBM per device.

v0:
```python
import functools
import math

import jax
import jax.numpy as jnp
from jax import lax
from jax.experimental import pallas as pl
from jax.experimental.pallas import tpu as pltpu
from jax.sharding import PartitionSpec as P

H = 8
KV = 4
FF = 9216
NEWTON_STEPS = 5
UPDATE_STEP = 10

NORM_EPS = 1e-06
SOFT_CAP = 50.0
MUON_RATE = 0.2
MUON_DECAY = 0.01
MUON_BETA = 0.95
ADAM_RATE = 0.3
BETA_ONE = 0.9
BETA_TWO = 0.95
ADAM_EPS = 1e-08
NEWTON_LINEAR = 3.4445
NEWTON_SQUARE = -4.775
NEWTON_CUBIC = 2.0315
NEWTON_PRECISION = lax.Precision.HIGH

BF16 = jnp.bfloat16
F32 = jnp.float32
VMEM_LIMIT = 62 * 1024 * 1024
NN = (((1,), (0,)), ((), ()))
NT = (((1,), (1,)), ((), ()))
TN = (((0,), (0,)), ((), ()))


def mm(a, b, dims):
    return lax.dot_general(a, b, dims, preferred_element_type=F32)


def rms_scale(rows, gain):
    inverse = lax.rsqrt(jnp.mean(rows * rows, axis=-1, keepdims=True) + NORM_EPS)
    return rows * inverse * gain


class Flow:
    def __init__(self, steps):
        self.steps = steps
        self.value = None
        self.sends = None
        self.advance(None)

    def advance(self, arrived):
        try:
            self.sends = self.steps.send(arrived)
        except StopIteration as stop:
            self.sends = None
            self.value = stop.value


def stage(flows, extra=(), idle=()):
    flows = [flow for flow in flows if flow.sends is not None]
    idle = [flow for flow in idle if flow.sends is not None and flow not in flows]
    arrived = [[lax.ppermute(*send) for send in flow.sends] for flow in flows]
    held = [[send[0] for send in flow.sends] for flow in idle]
    arrived, held, extra = lax.optimization_barrier((arrived, held, list(extra)))
    for flow, got in zip(flows, arrived):
        flow.advance(got)
    for flow, kept in zip(idle, held):
        flow.sends = [(value,) + send[1:] for value, send in zip(kept, flow.sends)]
    return extra


def run(steps):
    flow = Flow(steps)
    while flow.sends is not None:
        flow.advance([lax.ppermute(*send) for send in flow.sends])
    return flow.value


def finish(*flows):
    while any(flow.sends is not None for flow in flows):
        stage(flows)


def swap(value, axis, mask):
    size = lax.axis_size(axis)
    return (value, axis, [(i, i ^ mask) for i in range(size)])


def head_gather(rows):
    (other,) = yield [swap(rows, "head", 2)]
    pair = jnp.concatenate([rows, other], axis=0)
    (other,) = yield [swap(pair, "head", 1)]
    return jnp.concatenate([pair, other], axis=0)


def wide_gather(rows):
    (other,) = yield [swap(rows, "dp", 4)]
    both = jnp.concatenate([rows, other], axis=0)
    (other,) = yield [swap(both, "head", 2)]
    pair = jnp.concatenate([both, other], axis=0)
    (other,) = yield [swap(pair, "head", 1)]
    return [pair, other]


def add_low(kept, other):
    return (kept.astype(F32) + other.astype(F32)).astype(BF16)


def scatter_rows(kept, sent, moves, cuts=1):
    for k, (axis, mask) in enumerate(moves):
        last = k == len(moves) - 1
        others = []
        for piece in jnp.split(sent, cuts if last else 1):
            others += yield [swap(piece, axis, mask)]
        other = jnp.concatenate(others, axis=0) if len(others) > 1 else others[0]
        part = kept.astype(F32) + other.astype(F32)
        if not last:
            half = part.shape[0] // 2
            kept, sent = part[:half], part[half:].astype(BF16)
    return part


HEAD_MOVES = (("head", 1), ("head", 2))
WIDE_MOVES = (("head", 1), ("head", 2), ("dp", 4))


def total_sum(value):
    for axis in ("head", "dp"):
        mask = 1
        while mask < lax.axis_size(axis):
            (other,) = yield [swap(value, axis, mask)]
            value = value + other
            mask *= 2
    return value


class Ring:
    def __init__(self):
        size = lax.axis_size("dp")
        order = list(range(0, size, 2)) + list(range(size - 1, 0, -2))
        around = [[order[(order.index(i) + offset) % size] for offset in range(size)] for i in range(size)]
        self.size = size
        row = jnp.array(around, jnp.int32)[lax.axis_index("dp")]
        zero = jnp.zeros((), jnp.int32)
        self.around = [lax.select(lax.lt(row[k], zero), row[k] + size, row[k]) for k in range(size)]
        self.up = [(order[k], order[(k + 1) % size]) for k in range(size)]
        self.down = [(order[(k + 1) % size], order[k]) for k in range(size)]

    def index(self, offset, scale=1):
        return self.around[offset % self.size] * scale

    def gather(self, value, mid):
        half = self.size // 2
        out = jnp.zeros((self.size,) + value.shape, value.dtype)

        def put(out, piece, offset, start=0):
            spot = (self.index(offset), start) + (0,) * (value.ndim - 1)
            return lax.dynamic_update_slice(out, piece[None], spot, allow_negative_indices=False)

        out = put(out, value, 0)
        ahead, back = value, value
        for step in range(1, half):
            ahead, back = yield [(ahead, "dp", self.up), (back, "dp", self.down)]
            out = put(put(out, ahead, -step), back, step)
        if mid is None:
            (last,) = yield [(ahead, "dp", self.up)]
            return put(out, last, half)
        first, second = yield [(ahead[:mid], "dp", self.up), (back[mid:], "dp", self.down)]
        return put(put(out, first, half), second, half, mid)

    def part(self, array, axis, size=None):
        if size is None:
            return lambda offset: lax.dynamic_index_in_dim(
                array, self.index(offset), axis, keepdims=False, allow_negative_indices=False
            )
        return lambda offset: lax.dynamic_slice_in_dim(
            array, self.index(offset, size), size, axis, allow_negative_indices=False
        )

    def scatter(self, take, mid):
        half = self.size // 2
        far = take(half)
        kind = far.dtype
        if mid is None:
            (up,) = yield [(far, "dp", self.up)]
            down = None
        else:
            up, down = yield [(far[:mid], "dp", self.up), (far[mid:], "dp", self.down)]
        for step in range(half - 1, 0, -1):
            ahead, back = take(step).astype(F32), take(-step).astype(F32)
            if mid is None or step < half - 1:
                ahead = ahead + up
                back = back if down is None else back + down
            else:
                ahead = jnp.concatenate([ahead[:mid] + up, ahead[mid:]])
                back = jnp.concatenate([back[:mid], back[mid:] + down])
            up, down = yield [(ahead.astype(kind), "dp", self.up), (back.astype(kind), "dp", self.down)]
        return take(0).astype(F32) + up.astype(F32) + down.astype(F32)


def once(sends, take):
    def steps():
        take((yield sends))

    return Flow(steps())


SIDE_BIT = 2


def plane_classes():
    planes = range(lax.axis_size("dp") // 2)
    kept = [m for m in planes if m & 1 == 0]
    passed = [m for m in planes if m & 1 == 1]
    return {0: [0], 1: [1], 2: [m for m in passed if m != 1], 3: [m for m in kept if m]}


class Spread:
    def __init__(self, mine, other):
        self.mine, self.other = mine, other
        self.pieces = {0: mine}

    def move(self, moves):
        def take(arrived):
            for (_, _, _, number), piece in zip(moves, arrived):
                self.pieces[number] = piece

        return once([swap(value, "dp", offset << 1 | bit) for value, offset, bit, _ in moves], take)

    def cross(self):
        group = plane_classes()[3]
        return self.move([(self.other if m & SIDE_BIT else self.mine, m, 0, m << 1) for m in group])

    def near(self, key):
        group = plane_classes()[key]
        return self.move([(self.pieces[m << 1], 1, 0, (m ^ 1) << 1) for m in group])

    def y(self, key):
        group = plane_classes()[key]
        return self.move([(self.pieces[m << 1], 0, 1, m << 1 | 1) for m in group])

    def value(self):
        return [self.pieces[k] for k in range(lax.axis_size("dp"))]


class Reduce:
    def __init__(self, rows):
        self.rows = rows
        self.parts = {}
        self.sums = [[], []]

    def part(self, offset):
        terms = [term.astype(F32) for term in self.parts[offset]]
        return functools.reduce(jnp.add, terms)

    def hold(self, offset, *terms):
        self.parts.setdefault(offset, []).extend(terms)

    def y(self, key):
        group = plane_classes()[key]

        def take(arrived):
            for offset, got in zip(group, arrived):
                self.hold(offset, self.rows(offset << 1), got)

        return once([swap(self.rows(offset << 1 | 1), "dp", 1) for offset in group], take)

    def near(self, key):
        group = plane_classes()[key]

        def take(arrived):
            for offset, got in zip(group, arrived):
                self.hold(offset ^ 1, got)

        return once([swap(self.part(offset).astype(BF16), "dp", 2) for offset in group], take)

    def cross(self):
        group = plane_classes()[3]

        def take(arrived):
            for offset, got in zip(group, arrived):
                self.sums[1 if offset & SIDE_BIT else 0].append(got)

        return once([swap(self.part(offset).astype(BF16), "dp", offset << 1) for offset in group], take)

    def value(self):
        return self.parts[0] + self.sums[0], self.sums[1]


def params(**more):
    return pltpu.CompilerParams(vmem_limit_bytes=VMEM_LIMIT, **more)


TRIO = 3


def cast_blocks(blocks, count):
    _, r, c = blocks.shape

    def body(x_ref, o_ref):
        o_ref[...] = x_ref[...].astype(BF16)

    spec = pl.BlockSpec((TRIO, r, c), lambda k: (k, 0, 0))
    return pl.pallas_call(
        body,
        grid=(count // TRIO,),
        in_specs=[spec],
        out_specs=spec,
        out_shape=jax.ShapeDtypeStruct((count, r, c), BF16),
        compiler_params=params(),
        cost_estimate=pl.CostEstimate(flops=0, bytes_accessed=6 * count * r * c, transcendentals=0),
    )(blocks)


def pack_units(parity, blocks, first, kind_blocks, early):
    _, r, c = blocks.shape
    h = c // 2
    full = kind_blocks // 2
    each = kind_blocks // TRIO
    u, v = early * c, (full - early) * c + h

    def body(s_ref, *refs):
        parts, outs = refs[:each], refs[each:]

        def tile(f):
            return parts[f // TRIO].at[f % TRIO]

        for turn in range(2):

            @pl.when(s_ref[0] == turn)
            def _():
                for k in range(2):
                    side = turn ^ k
                    for i in range(full):
                        value = tile(side * full + i)[...].astype(BF16)
                        if i < early:
                            outs[2 * k][:, i * c : (i + 1) * c] = value
                        else:
                            outs[2 * k + 1][:, (i - early) * c : (i - early + 1) * c] = value
                    rest = tile(2 * full)[:, side * h : (side + 1) * h]
                    outs[2 * k + 1][:, v - h :] = rest.astype(BF16)

    def part(i):
        return pl.BlockSpec((TRIO, r, c), lambda k, s: (first // TRIO + each * k + i, 0, 0))

    wide = pl.BlockSpec((None, r, u), lambda k, s: (k, 0, 0))
    slim = pl.BlockSpec((None, r, v), lambda k, s: (k, 0, 0))
    shapes = [jax.ShapeDtypeStruct((3, r, u), BF16), jax.ShapeDtypeStruct((3, r, v), BF16)]
    return pl.pallas_call(
        body,
        grid_spec=pltpu.PrefetchScalarGridSpec(
            num_scalar_prefetch=1,
            grid=(3,),
            in_specs=[part(i) for i in range(each)],
            out_specs=[wide, slim, wide, slim],
        ),
        out_shape=shapes + shapes,
        compiler_params=params(),
        cost_estimate=pl.CostEstimate(flops=0, bytes_accessed=18 * kind_blocks * r * c, transcendentals=0),
    )(parity, *([blocks] * each))


def block_project(rows, blocks):
    t = rows.shape[0]
    count, d, c = blocks.shape

    def body(x_ref, w_ref, o_ref):
        o_ref[...] = mm(x_ref[...], w_ref[...], NN).astype(BF16)

    return pl.pallas_call(
        body,
        grid=(count,),
        in_specs=[
            pl.BlockSpec((t, d), lambda b: (0, 0)),
            pl.BlockSpec((None, d, c), lambda b: (b, 0, 0)),
        ],
        out_specs=pl.BlockSpec((None, t, c), lambda b: (b, 0, 0)),
        out_shape=jax.ShapeDtypeStruct((count, t, c), BF16),
        compiler_params=params(),
        cost_estimate=pl.CostEstimate(
            flops=2 * count * t * d * c, bytes_accessed=2 * (t * d + count * (d * c + t * c)), transcendentals=0
        ),
    )(rows, blocks)


def block_back(cols, blocks):
    count, t, c = cols.shape
    d = blocks.shape[1]
    half = t // 2

    def body(x_ref, w_ref, o_ref, p_ref, acc_ref):
        b = pl.program_id(0)

        @pl.when(b == 0)
        def _():
            acc_ref[...] = jnp.zeros_like(acc_ref)

        acc_ref[...] += mm(x_ref[...], w_ref[...], NT)

        @pl.when(b == count - 1)
        def _():
            o_ref[...] = acc_ref[:half, :].astype(BF16)
            p_ref[...] = acc_ref[half:, :].astype(BF16)

    result = pl.BlockSpec((half, d), lambda b: (0, 0))
    return pl.pallas_call(
        body,
        grid=(count,),
        in_specs=[
            pl.BlockSpec((None, t, c), lambda b: (b, 0, 0)),
            pl.BlockSpec((None, d, c), lambda b: (b, 0, 0)),
        ],
        out_specs=[result, result],
        out_shape=[jax.ShapeDtypeStruct((half, d), BF16)] * 2,
        scratch_shapes=[pltpu.VMEM((t, d), F32)],
        compiler_params=params(),
        cost_estimate=pl.CostEstimate(
            flops=2 * count * t * d * c, bytes_accessed=2 * (t * d + count * (d * c + t * c)), transcendentals=0
        ),
    )(cols, blocks)


def block_outer(rows, cols, d):
    t = rows[0].shape[0]
    c = cols[0].shape[2]
    starts = [0]
    for col in cols:
        starts.append(starts[-1] + col.shape[0])
    count = len(rows)
    total = starts[-1]

    def body(*refs):
        o_ref, t_ref = refs[2 * count :]
        b = pl.program_id(0)
        for k in range(count):

            @pl.when(b == starts[k])
            def _():
                t_ref[...] = refs[k][...].T

            @pl.when((b >= starts[k]) & (b < starts[k + 1]))
            def _():
                o_ref[...] = mm(t_ref[...], refs[count + k][...], NN).astype(BF16)

    def col_at(k):
        return pl.BlockSpec((None, t, c), lambda b: (jnp.clip(b - starts[k], 0, starts[k + 1] - starts[k] - 1), 0, 0))

    return pl.pallas_call(
        body,
        grid=(total,),
        in_specs=[pl.BlockSpec((t, d), lambda b: (0, 0))] * count + [col_at(k) for k in range(count)],
        out_specs=pl.BlockSpec((None, d, c), lambda b: (b, 0, 0)),
        out_shape=jax.ShapeDtypeStruct((total, d, c), BF16),
        scratch_shapes=[pltpu.VMEM((d, t), BF16)],
        compiler_params=params(),
        cost_estimate=pl.CostEstimate(
            flops=2 * total * t * d * c,
            bytes_accessed=2 * (count * t * d + total * (d * c + t * c)),
            transcendentals=0,
        ),
    )(*rows, *cols)


def in_group(local, width, head_shift):
    quarter = width // 4
    low = jnp.bitwise_and(local, quarter - 1)
    one = jnp.where(jnp.bitwise_and(local, quarter) != 0, 2 * quarter, 0)
    two = jnp.where(jnp.bitwise_and(local, 2 * quarter) != 0, quarter, 0)
    return jnp.bitwise_xor(low + one + two, head_shift)


def key_position(block, width, head_shift, shape, axis):
    local = lax.broadcasted_iota(jnp.int32, shape, axis)
    return block * width + in_group(local, width, head_shift)


def attend(place, queries, keys_values, query_pos, first_pos, scale, p):
    m, e = queries.shape
    n = keys_values.shape[0]
    step = 256

    def body(place_ref, q_ref, kv_ref, pos_ref, first_ref, low_ref, full_ref, sum_ref, acc_ref, tot_ref):
        j = pl.program_id(0)

        @pl.when(j == 0)
        def _():
            acc_ref[...] = jnp.zeros_like(acc_ref)
            tot_ref[...] = jnp.zeros_like(tot_ref)

        @pl.when(j <= place_ref[0])
        def _():
            key_pos = key_position(j, p, place_ref[1], (1, p), 1)
            for r in range(0, m, step):
                rows = pl.ds(r, step)
                raw = mm(q_ref[rows, :], kv_ref[:p, :], NT)
                soft = SOFT_CAP * jnp.tanh(raw * (scale / SOFT_CAP))
                seen = (key_pos >= first_ref[rows, :]) & (key_pos <= pos_ref[rows, :])
                terms = jnp.where(seen, jnp.exp(soft), 0.0)
                tot_ref[rows, :] += jnp.sum(terms, axis=1, keepdims=True)
                acc_ref[rows, :] += mm(terms.astype(BF16), kv_ref[p:, :], NN)

        @pl.when(j == n - 1)
        def _():
            total = tot_ref[...]
            mixed = acc_ref[...] / total
            full_ref[...] = mixed
            low_ref[...] = mixed.astype(BF16)
            sum_ref[...] = total

    whole = lambda shape: pl.BlockSpec(shape, lambda j, s: (0, 0))
    return pl.pallas_call(
        body,
        grid_spec=pltpu.PrefetchScalarGridSpec(
            num_scalar_prefetch=1,
            grid=(n,),
            in_specs=[
                whole((m, e)),
                pl.BlockSpec((None, 2 * p, e), lambda j, s: (jnp.minimum(j, s[0]), 0, 0)),
                whole((m, 1)),
                whole((m, 1)),
            ],
            out_specs=[whole((m, e)), whole((m, e)), whole((m, 1))],
            scratch_shapes=[pltpu.VMEM((m, e), F32), pltpu.VMEM((m, 1), F32)],
        ),
        out_shape=[
            jax.ShapeDtypeStruct((m, e), BF16),
            jax.ShapeDtypeStruct((m, e), F32),
            jax.ShapeDtypeStruct((m, 1), F32),
        ],
        compiler_params=params(),
        cost_estimate=pl.CostEstimate(
            flops=4 * m * n * p * e, bytes_accessed=4 * n * p * e, transcendentals=2 * m * n * p
        ),
    )(place, queries, keys_values, query_pos, first_pos)


def attend_back(place, queries, grads, keys_values, inverse, delta, query_pos, first_pos, scale, p):
    m, e = queries.shape
    n = keys_values.shape[0]
    step = 256

    def body(
        place_ref, q_ref, g_ref, kv_ref, inv_ref, delta_ref, pos_ref, first_ref, dq_ref, dkv_ref, acc_ref, dk_ref, dv_ref
    ):
        j = pl.program_id(0)

        @pl.when(j == 0)
        def _():
            acc_ref[...] = jnp.zeros_like(acc_ref)

        @pl.when(j <= place_ref[0])
        def _():
            key_pos = key_position(j, p, place_ref[1], (p, 1), 0)
            for r in range(0, m, step):
                rows = pl.ds(r, step)
                raw = mm(kv_ref[:p, :], q_ref[rows, :], NT)
                capped = jnp.tanh(raw * (scale / SOFT_CAP))
                seen = (key_pos >= first_ref[:, rows]) & (key_pos <= pos_ref[:, rows])
                probs = jnp.where(seen, jnp.exp(SOFT_CAP * capped), 0.0) * inv_ref[:, rows]
                grad_probs = mm(kv_ref[p:, :], g_ref[rows, :], NT)
                grad_raw = probs * (grad_probs - delta_ref[:, rows]) * (1.0 - capped * capped)
                grad_low = grad_raw.astype(BF16)
                value_part = mm(probs.astype(BF16), g_ref[rows, :], NN)
                key_part = mm(grad_low, q_ref[rows, :], NN)
                if r == 0:
                    dv_ref[...] = value_part
                    dk_ref[...] = key_part
                else:
                    dv_ref[...] += value_part
                    dk_ref[...] += key_part
                acc_ref[rows, :] += mm(grad_low, kv_ref[:p, :], TN)
            dkv_ref[0] = dk_ref[...].astype(BF16)
            dkv_ref[1] = dv_ref[...].astype(BF16)

        @pl.when(j > place_ref[0])
        def _():
            dkv_ref[...] = jnp.zeros_like(dkv_ref)

        @pl.when(j == n - 1)
        def _():
            dq_ref[...] = (acc_ref[...] * scale).astype(BF16)

    whole = lambda shape: pl.BlockSpec(shape, lambda j, s: (0, 0))
    return pl.pallas_call(
        body,
        grid_spec=pltpu.PrefetchScalarGridSpec(
            num_scalar_prefetch=1,
            grid=(n,),
            in_specs=[
                whole((m, e)),
                whole((m, e)),
                pl.BlockSpec((None, 2 * p, e), lambda j, s: (jnp.minimum(j, s[0]), 0, 0)),
                whole((1, m)),
                whole((1, m)),
                whole((1, m)),
                whole((1, m)),
            ],
            out_specs=[whole((m, e)), pl.BlockSpec((None, 2, p, e), lambda j, s: (j, 0, 0, 0))],
            scratch_shapes=[pltpu.VMEM((m, e), F32), pltpu.VMEM((p, e), F32), pltpu.VMEM((p, e), F32)],
        ),
        out_shape=[jax.ShapeDtypeStruct((m, e), BF16), jax.ShapeDtypeStruct((n, 2, p, e), BF16)],
        compiler_params=params(),
        cost_estimate=pl.CostEstimate(
            flops=10 * m * n * p * e, bytes_accessed=8 * n * p * e, transcendentals=2 * m * n * p
        ),
    )(place, queries, grads, keys_values, inverse, delta, query_pos, first_pos)


def gelu_pair(gate):
    outer = math.sqrt(2.0 / math.pi)
    square = gate * gate
    bent = jnp.tanh(outer * gate * (1.0 + 0.044715 * square))
    half = 0.5 * (1.0 + bent)
    slope = half + 0.5 * gate * (1.0 - bent * bent) * outer * (1.0 + 3.0 * 0.044715 * square)
    return gate * half, slope


def ffn_front(place, rows, cots, early, late):
    part_rows, d = rows[0].shape
    t = 2 * part_rows
    count = len(early)
    r = early[0].shape[1]
    u, v = early[0].shape[2], late[0].shape[2]
    tall = min(512, t)
    wide = d // 3
    cuts = [(k, min(256, u + v - k)) for k in range(0, u + v, 256)]

    def body(place_ref, x0, x1, y0, y1, *refs):
        early_refs, late_refs = refs[:count], refs[count : 2 * count]
        refs = refs[2 * count :]
        hs_ref, w_out = refs[:2]
        grad_refs = refs[2 : 2 + count], refs[2 + count : 2 + 2 * count]
        x, y, w, xt, yt, hs, row_sems, sems, out_sems, grad_sems = refs[2 + 2 * count :]
        row_copies = []
        for k, (source, target) in enumerate(((x0, x), (x1, x), (y0, y), (y1, y))):
            target = target.at[pl.ds((k % 2) * part_rows, part_rows), :]
            row_copies.append(pltpu.make_async_copy(source, target, row_sems.at[k]))
            row_copies[k].start()
        copies = []
        chunks = ((early_refs, pl.ds(0, u)), (late_refs, pl.ds(u, v)))

        def spot(k):
            return pl.ds(pl.multiple_of(jnp.bitwise_xor(place_ref[0], k) * r, 16) if count > 1 else 0, r)

        for k in range(count):
            for way, (sources, lanes) in enumerate(chunks):
                copy = pltpu.make_async_copy(sources[k], w.at[:, spot(k), lanes], sems.at[way, k])
                copy.start()
                copies.append(copy)
        for copy in row_copies:
            copy.wait()

        @pl.loop(0, d // 256)
        def _(k):
            cols = pl.ds(pl.multiple_of(k * 256, 256), 256)
            xt[cols, :] = x[:, cols].T
            yt[cols, :] = y[:, cols].T

        for copy in copies:
            copy.wait()
        kept = pltpu.make_async_copy(w, w_out, out_sems.at[0])
        kept.start()

        @pl.loop(0, t // tall)
        def _(i):
            part = pl.ds(pl.multiple_of(i * tall, tall), tall)
            for start, size in cuts:
                units = pl.ds(start, size)
                gate = mm(x[part, :], w[0, :, units], NN)
                up = mm(x[part, :], w[1, :, units], NN)
                grad = mm(y[part, :], w[2, :, units], NN)
                active, slope = gelu_pair(gate)
                hs[0, part, units] = (active * up).astype(BF16)
                hs[1, part, units] = (grad * up * slope).astype(BF16)
                hs[2, part, units] = (grad * active).astype(BF16)

        sides = pltpu.make_async_copy(hs, hs_ref, out_sems.at[1])
        sides.start()
        kept.wait()
        copies = []
        for kind, (left, right) in enumerate(((xt, 1), (xt, 2), (yt, 0))):

            @pl.loop(0, d // wide)
            def _(k):
                cols = pl.ds(pl.multiple_of(k * wide, wide), wide)
                w[kind, cols, :] = mm(left[cols, :], hs[right], NN).astype(BF16)

            for k in range(count):
                for way, (_, lanes) in enumerate(chunks):
                    target = grad_refs[way][k].at[kind]
                    copy = pltpu.make_async_copy(w.at[kind, spot(k), lanes], target, grad_sems.at[kind, way, k])
                    copy.start()
                    copies.append(copy)
        sides.wait()
        for copy in copies:
            copy.wait()

    apart = pl.BlockSpec(memory_space=pl.ANY)
    return pl.pallas_call(
        body,
        grid_spec=pltpu.PrefetchScalarGridSpec(
            num_scalar_prefetch=1,
            grid=(1,),
            in_specs=[apart] * (4 + 2 * count),
            out_specs=[apart] * (2 + 2 * count),
            scratch_shapes=[
                pltpu.VMEM((t, d), BF16),
                pltpu.VMEM((t, d), BF16),
                pltpu.VMEM((3, d, u + v), BF16),
                pltpu.VMEM((d, t), BF16),
                pltpu.VMEM((d, t), BF16),
                pltpu.VMEM((3, t, u + v), BF16),
                pltpu.SemaphoreType.DMA((4,)),
                pltpu.SemaphoreType.DMA((2, count)),
                pltpu.SemaphoreType.DMA((2,)),
                pltpu.SemaphoreType.DMA((3, 2, count)),
            ],
        ),
        out_shape=[
            jax.ShapeDtypeStruct((3, t, u + v), BF16),
            jax.ShapeDtypeStruct((3, d, u + v), BF16),
            *[jax.ShapeDtypeStruct((3, r, u), BF16)] * count,
            *[jax.ShapeDtypeStruct((3, r, v), BF16)] * count,
        ],
        compiler_params=params(),
        cost_estimate=pl.CostEstimate(
            flops=12 * t * d * (u + v), bytes_accessed=12 * d * (u + v) + 4 * t * d, transcendentals=t * (u + v)
        ),
    )(place, *rows, *cots, *early, *late)


def ffn_back(sides, blocks):
    _, t, u = sides.shape
    d = blocks.shape[1]
    wide = 256
    half = t // 2

    def body(s_ref, w_ref, *refs):
        for k in range(2):
            part = pl.ds(k * half, half)
            refs[k][...] = mm(s_ref[0, part, :], w_ref[2], NT).astype(BF16)
            refs[2 + k][...] = (mm(s_ref[1, part, :], w_ref[0], NT) + mm(s_ref[2, part, :], w_ref[1], NT)).astype(BF16)

    return pl.pallas_call(
        body,
        grid=(d // wide,),
        in_specs=[
            pl.BlockSpec((3, t, u), lambda k: (0, 0, 0), pipeline_mode=pl.Buffered(1)),
            pl.BlockSpec((3, wide, u), lambda k: (0, k, 0)),
        ],
        out_specs=[pl.BlockSpec((half, wide), lambda k: (0, k))] * 4,
        out_shape=[jax.ShapeDtypeStruct((half, d), BF16)] * 4,
        compiler_params=params(),
        cost_estimate=pl.CostEstimate(
            flops=6 * t * d * u, bytes_accessed=6 * d * u + 6 * t * u + 4 * t * d, transcendentals=0
        ),
    )(sides, blocks)


def gram_parts(m):
    h = m.shape[1] // 2
    high = m.astype(BF16)
    low = (m - high.astype(F32)).astype(BF16)
    mixed = mm(high, low, TN)
    gram = mm(high, high, TN) + mm(low, low, TN) + mixed + mixed.T
    return gram[:h, :h], gram[:h, h:], gram[h:, h:]


def ffn_moment(parity, own, other, momentum, first, blocks, places):
    total, r, c = momentum.shape
    terms = [*own, *other]
    counts = [len(group) for group in terms]
    u, v = own[0][0].shape[2], own[1][0].shape[2]
    early = u // c
    h = c // 2
    full = early + 1
    each = blocks // TRIO

    def body(s_ref, *refs):
        groups = []
        for count in counts:
            groups.append(refs[:count])
            refs = refs[count:]
        m_ref, wg_ref, nm_ref, gram_ref = refs
        j = pl.program_id(0)

        def total_of(group, start, size):
            lanes = pl.ds(start, size)
            return functools.reduce(jnp.add, [ref[:, lanes].astype(F32) for ref in group])

        @pl.when(j >= TRIO * each)
        def _():
            gram_ref[...] = jnp.zeros_like(gram_ref)

        for turn in range(each):
            for mine in range(2):

                @pl.when((j < TRIO * each) & (lax.rem(j, each) == turn) & (s_ref[0] == mine))
                def _():
                    for i in range(TRIO):
                        side, f = divmod(turn * TRIO + i, full)
                        if side == 2:
                            for k in range(2):
                                group = groups[1 if k == mine else 3]
                                wg_ref[i, :, k * h : (k + 1) * h] = total_of(group, c, h)
                        elif f < early:
                            wg_ref[i] = total_of(groups[0 if side == mine else 2], f * c, c)
                        else:
                            wg_ref[i] = total_of(groups[1 if side == mine else 3], 0, c)

        @pl.when(j < TRIO * each)
        def _():
            for i in range(TRIO):
                new = MUON_BETA * m_ref[i] + wg_ref[i]
                nm_ref[i] = new
                gram_ref[i, 0], gram_ref[i, 1], gram_ref[i, 2] = gram_parts(new)

    kind = lambda j, s: (jnp.minimum(j // each, 2), 0, 0)
    block = lambda j, s: (first // TRIO + jnp.minimum(j, TRIO * each - 1), 0, 0)
    arrays = [array for group in terms for array in group]
    return pl.pallas_call(
        body,
        grid_spec=pltpu.PrefetchScalarGridSpec(
            num_scalar_prefetch=1,
            grid=(places // TRIO,),
            in_specs=[pl.BlockSpec((None,) + array.shape[1:], kind) for array in arrays]
            + [pl.BlockSpec((TRIO, r, c), block)],
            out_specs=[
                pl.BlockSpec((TRIO, r, c), block),
                pl.BlockSpec((TRIO, r, c), block),
                pl.BlockSpec((TRIO, 3, h, h), lambda j, s: (j, 0, 0, 0)),
            ],
        ),
        out_shape=[
            jax.ShapeDtypeStruct((total, r, c), F32),
            jax.ShapeDtypeStruct((total, r, c), F32),
            jax.ShapeDtypeStruct((places, 3, h, h), F32),
        ],
        compiler_params=params(),
        cost_estimate=pl.CostEstimate(
            flops=6 * 3 * blocks * r * c * c, bytes_accessed=16 * 3 * blocks * r * c, transcendentals=0
        ),
    )(parity, *arrays, momentum)


def attn_moment(grads, pairs, momentum, weight_grads, new_momentum):
    count, r, c = grads.shape
    h = c // 2

    def body(s_ref, g_ref, m_ref, wg_in, nm_in, wg_ref, nm_ref, gram_ref):
        for i in range(2):
            new = MUON_BETA * m_ref[i] + g_ref[i]
            wg_ref[i] = g_ref[i]
            nm_ref[i] = new
            gram_ref[i, 0], gram_ref[i, 1], gram_ref[i, 2] = gram_parts(new)

    block = pl.BlockSpec((2, r, c), lambda j, s: (s[j], 0, 0))
    apart = pl.BlockSpec(memory_space=pl.ANY)
    return pl.pallas_call(
        body,
        grid_spec=pltpu.PrefetchScalarGridSpec(
            num_scalar_prefetch=1,
            grid=(count // 2,),
            in_specs=[pl.BlockSpec((2, r, c), lambda j, s: (j, 0, 0)), block, apart, apart],
            out_specs=[block, block, pl.BlockSpec((2, 3, h, h), lambda j, s: (j, 0, 0, 0))],
        ),
        out_shape=[
            jax.ShapeDtypeStruct(momentum.shape, F32),
            jax.ShapeDtypeStruct(momentum.shape, F32),
            jax.ShapeDtypeStruct((count, 3, h, h), F32),
        ],
        input_output_aliases={3: 0, 4: 1},
        compiler_params=params(),
        cost_estimate=pl.CostEstimate(
            flops=6 * count * r * c * c, bytes_accessed=16 * count * r * c, transcendentals=0
        ),
    )(jnp.array(pairs, jnp.int32), grads, momentum, weight_grads, new_momentum)


def renew(weights, momentum, factors, spots, updated):
    _, r, c = weights.shape
    h = c // 2
    steps = len(spots)
    table = jnp.array([spot for spot, _ in spots] + [f for _, places in spots for f in places], jnp.int32)

    def body(s_ref, w_ref, m_ref, *refs):
        factor_refs, o_ref = refs[:TRIO], refs[-1]
        for i in range(TRIO):
            left = m_ref[i, :, :h].astype(BF16)
            right = m_ref[i, :, h:].astype(BF16)
            first, off, last = factor_refs[i][0], factor_refs[i][1], factor_refs[i][2]
            start = mm(left, first, NN) + mm(right, off, NT)
            rest = mm(left, off, NN) + mm(right, last, NN)
            keep = 1.0 - MUON_RATE * MUON_DECAY
            o_ref[i, :, :h] = w_ref[i, :, :h] * keep - MUON_RATE * start
            o_ref[i, :, h:] = w_ref[i, :, h:] * keep - MUON_RATE * rest

    block = pl.BlockSpec((TRIO, r, c), lambda j, s: (s[j], 0, 0))

    def factor_at(i):
        return pl.BlockSpec((None, 3, h, h), lambda j, s: (s[steps + TRIO * j + i], 0, 0, 0))

    apart = [pl.BlockSpec(memory_space=pl.ANY)] * len(updated)
    return pl.pallas_call(
        body,
        grid_spec=pltpu.PrefetchScalarGridSpec(
            num_scalar_prefetch=1,
            grid=(steps,),
            in_specs=[block, block] + [factor_at(i) for i in range(TRIO)] + apart,
            out_specs=block,
        ),
        out_shape=jax.ShapeDtypeStruct(weights.shape, F32),
        input_output_aliases={3 + TRIO: 0} if updated else {},
        compiler_params=params(),
        cost_estimate=pl.CostEstimate(
            flops=2 * TRIO * steps * r * c * c, bytes_accessed=12 * TRIO * steps * r * c, transcendentals=0
        ),
    )(table, weights, momentum, *([factors] * TRIO), *updated)


def top(spec, a, b):
    return jnp.einsum(spec, a, b, precision=NEWTON_PRECISION)


def newton_factor(grams, growth):
    size = grams.shape[-1]
    eye = jnp.eye(size, dtype=F32)
    norm = jnp.sqrt(jnp.sum(grams * eye, axis=(1, 2), keepdims=True))
    inverse = 1.0 / (norm + 1e-07)
    gram = grams * (inverse * inverse)
    factor = None
    for sweep in range(NEWTON_STEPS):
        square = top("bij,bjk->bik", gram, gram)
        poly = NEWTON_LINEAR * eye + NEWTON_SQUARE * gram + NEWTON_CUBIC * square
        factor = poly if sweep == 0 else top("bij,bjk->bik", factor, poly)
        if sweep < NEWTON_STEPS - 1:
            gram = top("bij,bjk->bik", top("bij,bjk->bik", gram, poly), poly)
    return factor * (growth * inverse)


def fold(squares):
    h = squares.shape[1] // 2
    return jnp.stack([squares[:, :h, :h], squares[:, :h, h:], squares[:, h:, h:]], axis=1)


def unfold(parts):
    first, off, last = parts[:, 0], parts[:, 1], parts[:, 2]
    upper = jnp.concatenate([first, off], axis=2)
    lower = jnp.concatenate([jnp.swapaxes(off, 1, 2), last], axis=2)
    return jnp.concatenate([upper, lower], axis=1)


def gram_sums(ring, parts, cap):
    h = parts.shape[2]
    parts = parts.reshape(-1, h, h)
    rows = 3 * cap
    mine = yield from ring.scatter(ring.part(parts, 0, rows), rows // 2 if cap > 1 else None)
    return unfold(mine.reshape(cap, 3, h, h))


def all_factors(ring, factors):
    cap, c, _ = factors.shape
    parts = fold(factors.astype(BF16)).reshape(3 * cap, c // 2, c // 2)
    parts = yield from ring.gather(parts, 3 * cap // 2 if cap > 1 else None)
    return parts.reshape(ring.size * cap, 3, c // 2, c // 2)


def on_device(block_in, cotangent, seq_ids, weights, momentum, gains, gain_first, gain_second):
    tok_rows, model_width = block_in.shape
    rows_dp, group_blocks, head_dim = weights.shape
    head_count = lax.axis_size("head")
    data_count = lax.axis_size("dp")
    group_rows = tok_rows * head_count
    key_heads = KV // head_count
    query_heads = H // head_count
    ffn_blocks = FF // (head_dim * head_count)
    out_mark = query_heads + 2 * key_heads
    gate_mark = out_mark + query_heads
    half_dim = head_dim // 2
    full = ffn_blocks // 2
    scale = head_dim ** (-0.5)
    growth = math.sqrt(max(1.0, model_width / head_dim))
    data_index = lax.axis_index("dp")
    head_index = lax.axis_index("head")
    parity = (data_index >> 2) & 1
    ring = Ring()

    weights = jnp.transpose(weights, (1, 0, 2))
    momentum = jnp.transpose(momentum, (1, 0, 2))
    attn_low = cast_blocks(weights, gate_mark)
    inputs = block_in.astype(F32)
    normed_one, norm_one_back = jax.vjp(rms_scale, inputs, gains[0])
    ids_column = jnp.pad(seq_ids.astype(BF16)[:, None], ((0, 0), (0, 127)))

    early = full - 1
    mine_early, mine_late, other_early, other_late = pack_units(
        jnp.reshape(parity, (1,)), weights, gate_mark, ffn_blocks, early
    )
    spread = [Spread(mine_early, other_early), Spread(mine_late, other_late)]

    group_in = run(head_gather(jnp.concatenate([normed_one.astype(BF16), ids_column], axis=1)))
    qkv_parts = run(ring.gather(attn_low[:out_mark], out_mark // 2))
    qkv_blocks = jnp.transpose(qkv_parts, (1, 0, 2, 3)).reshape(out_mark, model_width, head_dim)
    cot_flow = Flow(wide_gather(cotangent))
    group_in, qkv_blocks, attn_low = stage(
        [spread[0].near(0), spread[0].y(0)], [group_in, qkv_blocks, attn_low], idle=[cot_flow]
    )
    projected = block_project(group_in, qkv_blocks)
    queries = projected[:query_heads].reshape(query_heads * group_rows, head_dim)
    group_ids = group_in[:, model_width]
    kv_rows = 2 * key_heads * group_rows
    out_rows = query_heads * rows_dp
    id_rows = group_rows // head_dim
    packed = jnp.concatenate(
        [
            projected[query_heads:].reshape(kv_rows, head_dim),
            attn_low[out_mark:].reshape(out_rows, head_dim),
            jnp.pad(group_ids.reshape(id_rows, head_dim), ((0, 16 - id_rows), (0, 0))),
        ],
        axis=0,
    )
    keys_values = run(ring.gather(packed, packed.shape[0] // 32 * 16))
    out_blocks = keys_values[:, kv_rows : kv_rows + out_rows].reshape(data_count, query_heads, rows_dp, head_dim)
    out_blocks = jnp.transpose(out_blocks, (1, 0, 2, 3)).reshape(query_heads, model_width, head_dim)
    queries, keys_values, out_blocks = stage(
        [cot_flow, spread[0].y(1), spread[1].near(0)], [queries, keys_values, out_blocks]
    )
    all_ids = keys_values[:, kv_rows + out_rows : kv_rows + out_rows + id_rows].reshape(-1)

    local = in_group(jnp.arange(group_rows, dtype=jnp.int32), group_rows, head_index * tok_rows)
    query_pos = data_index * group_rows + local
    first_pos = jnp.sum((all_ids[None, :] < group_ids[:, None]).astype(jnp.int32), axis=1)
    query_pos = jnp.tile(query_pos, query_heads)
    first_pos = jnp.tile(first_pos, query_heads)
    place = jnp.stack([data_index, head_index * tok_rows]).astype(jnp.int32)
    mixed_low, mixed_full, totals = attend(
        place, queries, keys_values, query_pos[:, None], first_pos[:, None], scale, group_rows
    )
    mixed_heads = mixed_low.reshape(query_heads, group_rows, head_dim)
    mixed_heads, mixed_full, totals, attn_part = stage(
        [spread[0].cross(), spread[1].y(0), spread[1].y(1), cot_flow],
        [mixed_heads, mixed_full, totals, block_back(mixed_heads, out_blocks)],
    )
    attn_flow = Flow(scatter_rows(*attn_part, HEAD_MOVES))
    attn_flow.advance([lax.ppermute(*send) for send in attn_flow.sends])
    stage([attn_flow, spread[0].near(3), spread[0].y(3), spread[1].cross()], idle=[cot_flow])
    residual = inputs + attn_flow.value
    normed_two, norm_two_back = jax.vjp(rms_scale, residual, gains[1])
    wide_flow = Flow(wide_gather(normed_two.astype(BF16)))
    stage([wide_flow, spread[0].y(2), spread[1].near(3), spread[1].y(3)], idle=[cot_flow])
    stage([wide_flow, spread[1].y(2), cot_flow])
    stage([wide_flow])
    finish(wide_flow, cot_flow)

    def whole_rows(pieces):
        if rows_dp % 16 == 0:
            return pieces
        out = jnp.zeros((3, data_count) + pieces[0].shape[1:], BF16)
        for k, piece in enumerate(pieces):
            out = lax.dynamic_update_index_in_dim(out, piece, data_index ^ k, 1)
        return [out.reshape(3, model_width, -1)]

    ffn_sides, ffn_full, *ffn_grads = ffn_front(
        place, wide_flow.value, cot_flow.value, whole_rows(spread[0].value()), whole_rows(spread[1].value())
    )

    def taker(pieces):
        if len(pieces) > 1:
            return lambda k: pieces[k]
        cut = pieces[0].reshape(3, data_count, rows_dp, pieces[0].shape[2])
        return lambda k: lax.dynamic_index_in_dim(cut, data_index ^ k, 1, keepdims=False)

    pieces = len(ffn_grads) // 2
    reduce = [Reduce(taker(ffn_grads[:pieces])), Reduce(taker(ffn_grads[pieces:]))]
    *down_part, dx_kept, dx_sent = stage([reduce[0].y(2)], ffn_back(ffn_sides, ffn_full))
    out_flow = Flow(scatter_rows(*down_part, WIDE_MOVES, 4))
    dx_flow = Flow(scatter_rows(dx_kept, dx_sent, WIDE_MOVES))
    dx_flow.advance([lax.ppermute(*send) for send in dx_flow.sends])
    stage([dx_flow, reduce[0].near(2), reduce[0].y(3), reduce[1].y(2)])
    stage([dx_flow, reduce[1].y(3), reduce[1].y(1), reduce[1].near(2), out_flow])
    grad_residual_norm, grad_gain_two = norm_two_back(dx_flow.value)
    grad_residual = cotangent.astype(F32) + grad_residual_norm
    grad_flow = Flow(head_gather(grad_residual.astype(BF16)))
    stage([grad_flow, reduce[1].cross(), reduce[0].y(1)])
    grad_flow.advance([lax.ppermute(*send) for send in grad_flow.sends])
    group_grad = grad_flow.value

    grad_heads = block_project(group_grad, out_blocks)
    grad_mixed = grad_heads.reshape(query_heads * group_rows, head_dim)
    delta = jnp.sum(grad_mixed.astype(F32) * mixed_full, axis=1)
    grad_queries, grad_keys_values = attend_back(
        place,
        queries,
        grad_mixed,
        keys_values,
        1.0 / totals.reshape(1, -1),
        delta[None, :],
        query_pos[None, :],
        first_pos[None, :],
        scale,
        group_rows,
    )
    late_near = reduce[1].near(1)
    group_grad, grad_queries, grad_keys_values = stage(
        [reduce[0].cross(), reduce[0].near(1), reduce[0].y(0), reduce[1].y(0)],
        [group_grad, grad_queries, grad_keys_values],
        idle=[late_near, out_flow],
    )
    grad_queries = grad_queries.reshape(query_heads, group_rows, head_dim)

    late = 2
    main = 3 * ffn_blocks - late
    cap = -(-main // data_count)
    places = -(-max(cap * data_count, 3 * ffn_blocks) // TRIO) * TRIO
    def weight_sums(outer):
        cut = outer.reshape(outer.shape[0], data_count, rows_dp, head_dim)
        return Flow(ring.scatter(ring.part(cut, 1), outer.shape[0] // 2 if outer.shape[0] > 2 else None))

    key_flow = Flow(ring.scatter(ring.part(grad_keys_values, 0), key_heads))
    (outer,) = stage(
        [key_flow, late_near, out_flow],
        [block_outer([group_in, group_grad], [grad_queries, mixed_heads], model_width)],
    )
    (own_early, other_early), (own_late, other_late) = (part.value() for part in reduce)
    first_flow = weight_sums(outer)
    weight_grads, new_momentum, grams = stage(
        [key_flow, first_flow],
        ffn_moment(
            jnp.reshape(parity, (1,)),
            [own_early, own_late],
            [other_early, other_late],
            momentum,
            gate_mark,
            ffn_blocks,
            places,
        ),
    )
    gram_flow = Flow(gram_sums(ring, grams, cap))
    stage([key_flow, first_flow, gram_flow])
    while key_flow.sends is not None:
        stage([key_flow, first_flow, gram_flow])
    key_value_sums = key_flow.value
    grad_keys = (key_value_sums[:key_heads] * scale).astype(BF16)
    grad_values = key_value_sums[key_heads:].astype(BF16)
    grad_keys_values = jnp.concatenate([grad_keys, grad_values], axis=0)
    (outer,) = stage([first_flow, gram_flow, out_flow], [block_outer([group_in], [grad_keys_values], model_width)])
    finish(first_flow)
    second_flow = weight_sums(outer)
    pairs = [k for k in range(gate_mark // 2) if not query_heads <= 2 * k < out_mark]
    grad_projected = jnp.concatenate([grad_queries, grad_keys_values], axis=0)
    *attn_dx, weight_grads, new_momentum, first_grams = stage(
        [second_flow, gram_flow],
        [
            *block_back(grad_projected, qkv_blocks),
            *attn_moment(first_flow.value, pairs, momentum, weight_grads, new_momentum),
        ],
    )
    last_flow = Flow(scatter_rows(*attn_dx, HEAD_MOVES))
    finish(gram_flow)
    gram_value = gram_flow.value
    while second_flow.sends is not None:
        (gram_value,) = stage([second_flow, last_flow, out_flow], [gram_value])
    finish(last_flow, out_flow)
    block_out = (residual + out_flow.value).astype(BF16)
    grad_input_norm, grad_gain_one = norm_one_back(last_flow.value)
    grad_input = grad_residual + grad_input_norm
    gain_flow = Flow(total_sum(jnp.stack([grad_gain_one, grad_gain_two])))
    weight_grads, new_momentum, second_grams = attn_moment(
        second_flow.value, list(range(query_heads // 2, out_mark // 2)), momentum, weight_grads, new_momentum
    )
    late_count = gate_mark + late
    late_cap = -(-late_count // data_count)
    late_grams = jnp.concatenate([first_grams, second_grams, grams[main : main + late]], axis=0)
    late_grams = jnp.pad(late_grams, ((0, late_cap * data_count - late_count), (0, 0), (0, 0), (0, 0)))
    late_gram_flow = Flow(gram_sums(ring, late_grams, late_cap))
    (gram_value,) = stage([late_gram_flow, gain_flow], [gram_value])
    (factors,) = stage([late_gram_flow, gain_flow], [newton_factor(gram_value, growth)])
    factor_flow = Flow(all_factors(ring, factors))
    while late_gram_flow.sends is not None:
        stage([late_gram_flow, factor_flow, gain_flow])
    (late_factors,) = stage([factor_flow, gain_flow], [newton_factor(late_gram_flow.value, growth)])
    late_factor_flow = Flow(all_factors(ring, late_factors))
    while factor_flow.sends is not None:
        stage([factor_flow, late_factor_flow, gain_flow])
    factors = factor_flow.value

    threes = main // TRIO
    early_spots = [(gate_mark // TRIO + k, [TRIO * k + i for i in range(TRIO)]) for k in range(threes)]
    new_weights = []
    for k in range(0, threes, 3):
        new_weights = stage(
            [late_factor_flow, gain_flow],
            [renew(weights, new_momentum, factors, early_spots[k : k + 3], new_weights)],
        )

    finish(late_factor_flow, gain_flow)
    gain_grads = gain_flow.value
    rest = jnp.concatenate([late_factor_flow.value[:late_count], factors[TRIO * threes : main]], axis=0)
    blocks_of = [2 * pair + i for pair in pairs for i in range(2)] + list(range(query_heads, out_mark))
    blocks_of += [gate_mark + main + k for k in range(late)] + [gate_mark + k for k in range(TRIO * threes, main)]
    late_spots = [
        (spot, [blocks_of.index(TRIO * spot + i) for i in range(TRIO)])
        for spot in sorted({block // TRIO for block in blocks_of})
    ]
    new_weights = renew(weights, new_momentum, rest, late_spots, new_weights)

    new_gain_first = BETA_ONE * gain_first + (1.0 - BETA_ONE) * gain_grads
    new_gain_second = BETA_TWO * gain_second + (1.0 - BETA_TWO) * gain_grads * gain_grads
    first_hat = new_gain_first / (1.0 - BETA_ONE**UPDATE_STEP)
    second_hat = new_gain_second / (1.0 - BETA_TWO**UPDATE_STEP)
    new_gains = gains - ADAM_RATE * first_hat / (jnp.sqrt(second_hat) + ADAM_EPS)
    back = lambda array: jnp.transpose(array, (1, 0, 2))
    return (
        block_out,
        grad_input,
        back(weight_grads),
        back(new_momentum),
        back(new_weights),
        gain_grads,
        new_gain_first,
        new_gain_second,
        new_gains,
    )


def solution(mesh):
    return jax.shard_map(
        on_device,
        mesh=mesh,
        in_specs=(
            P(("dp", "head"), None),
            P(("dp", "head"), None),
            P(("dp", "head")),
            P("dp", "head", None),
            P("dp", "head", None),
            P(),
            P(),
            P(),
        ),
        out_specs=(
            P(("dp", "head"), None),
            P(("dp", "head"), None),
            P("dp", "head", None),
            P("dp", "head", None),
            P("dp", "head", None),
            P(),
            P(),
            P(),
            P(),
        ),
        check_vma=False,
    )
```

profile of v0, /device:TPU:0, one launch (start us, length us, event | category | flops | bytes accessed | tf_op | source)
XLA Modules:
  0.0 1005.0 jit_solution(14229595980359518118)
XLA Ops:
  7.9 6.0 shard_map.214
  45.4 17.0 %collective-permute-done.8 = bf16[4,288,256]{2,1,0:T(8,128)(2,1)S(1)} collective-permute-done((bf16[4,288,256]{2,1,0:T(8,128)(2,1)}, bf16[4,288,256]{2,1,0:T(8,128)(2,1)S(1)}, u32[]{:S(2)}, u32[]{:S(2)}) %collective-permute-start.8) | collective-permute-done | bytes 589856 | tf_op jit(solution)/shard_map/ppermute | solution.py:79
  68.1 8.8 collective-permute-done.10
  86.2 6.6 shard_map.216
  105.1 12.4 %collective-permute-done.17 = bf16[1616,256]{1,0:T(8,128)(2,1)} collective-permute-done((bf16[1616,256]{1,0:T(8,128)(2,1)}, bf16[1616,256]{1,0:T(8,128)(2,1)}, u32[]{:S(2)}, u32[]{:S(2)}) %collective-permute-start.17) | collective-permute-done | bytes 827424 | tf_op jit(solution)/shard_map/ppermute | solution.py:79
  118.9 10.1 %collective-permute-done.18 = bf16[1616,256]{1,0:T(8,128)(2,1)} collective-permute-done((bf16[1616,256]{1,0:T(8,128)(2,1)}, bf16[1616,256]{1,0:T(8,128)(2,1)}, u32[]{:S(2)}, u32[]{:S(2)}) %collective-permute-start.18) | collective-permute-done | bytes 827424 | tf_op jit(solution)/shard_map/ppermute | solution.py:79
  131.4 29.4 %collective-permute-done.19 = bf16[1616,256]{1,0:T(8,128)(2,1)S(1)} collective-permute-done((bf16[1616,256]{1,0:T(8,128)(2,1)}, bf16[1616,256]{1,0:T(8,128)(2,1)S(1)}, u32[]{:S(2)}, u32[]{:S(2)}) %collective-permute-start.19) | collective-permute-done | bytes 827424 | tf_op jit(solution)/shard_map/ppermute | solution.py:79
  163.0 16.3 %collective-permute-done.21 = bf16[1616,256]{1,0:T(8,128)(2,1)S(1)} collective-permute-done((bf16[1616,256]{1,0:T(8,128)(2,1)S(1)}, bf16[1616,256]{1,0:T(8,128)(2,1)S(1)}, u32[]{:S(2)}, u32[]{:S(2)}) %collective-permute-start.21) | collective-permute-done | bytes 827424 | tf_op jit(solution)/shard_map/ppermute | solution.py:79
  181.8 8.4 collective-permute-done.23
  191.6 12.8 %collective-permute-start = (bf16[3,288,768]{2,1,0:T(8,128)(2,1)}, bf16[3,288,768]{2,1,0:T(8,128)(2,1)}, u32[]{:S(2)}, u32[]{:S(2)}) collective-permute-start(bf16[3,288,768]{2,1,0:T(8,128)(2,1)} %get-tuple-element.198), channel_id=1, source_target_pairs={{0,16},{4,20},{8,24},{12,28},{16,0},{20,4},{24,8},{28,12},{1,17},{... | collective-permute-start | bytes 3981320 | tf_op jit(solution)/shard_map/ppermute | solution.py:66
  212.3 5.3 shard_map.217
  217.5 5.0 shard_map.218
  222.5 22.6 %collective-permute-done.refs_4_ = bf16[3,288,768]{2,1,0:T(8,128)(2,1)} collective-permute-done((bf16[3,288,768]{2,1,0:T(8,128)(2,1)}, bf16[3,288,768]{2,1,0:T(8,128)(2,1)}, u32[]{:S(2)}, u32[]{:S(2)}) %collective-permute-start) | collective-permute-done | bytes 1327136 | tf_op jit(solution)/shard_map/ppermute | solution.py:66
  252.8 23.5 %collective-permute-done.31.refs_12_ = bf16[3,288,384]{2,1,0:T(8,128)(2,1)S(1)} collective-permute-done((bf16[3,288,384]{2,1,0:T(8,128)(2,1)}, bf16[3,288,384]{2,1,0:T(8,128)(2,1)S(1)}, u32[]{:S(2)}, u32[]{:S(2)}) %collective-permute-start.31) | collective-permute-done | bytes 663584 | tf_op jit(solution)/shard_map/ppermute | solution.py:66
  276.3 15.0 %collective-permute-done.29.refs_6_ = bf16[3,288,768]{2,1,0:T(8,128)(2,1)S(1)} collective-permute-done((bf16[3,288,768]{2,1,0:T(8,128)(2,1)}, bf16[3,288,768]{2,1,0:T(8,128)(2,1)S(1)}, u32[]{:S(2)}, u32[]{:S(2)}) %collective-permute-start.29) | collective-permute-done | bytes 1327136 | tf_op jit(solution)/shard_map/ppermute | solution.py:66
  296.7 25.4 %collective-permute-done.32 = bf16[128,2304]{1,0:T(8,128)(2,1)S(1)} collective-permute-done((bf16[128,2304]{1,0:T(8,128)(2,1)S(1)}, bf16[128,2304]{1,0:T(8,128)(2,1)S(1)}, u32[]{:S(2)}, u32[]{:S(2)}) %collective-permute-start.32) | collective-permute-done | bytes 589856 | tf_op jit(solution)/shard_map/ppermute | solution.py:66
  322.1 14.3 %collective-permute-done.33.refs_7_ = bf16[3,288,768]{2,1,0:T(8,128)(2,1)S(1)} collective-permute-done((bf16[3,288,768]{2,1,0:T(8,128)(2,1)S(1)}, bf16[3,288,768]{2,1,0:T(8,128)(2,1)S(1)}, u32[]{:S(2)}, u32[]{:S(2)}) %collective-permute-start.33) | collective-permute-done | bytes 1327136 | tf_op jit(solution)/shard_map/ppermute | solution.py:66
  338.4 16.7 %collective-permute-done.37.refs_15_ = bf16[3,288,384]{2,1,0:T(8,128)(2,1)S(1)} collective-permute-done((bf16[3,288,384]{2,1,0:T(8,128)(2,1)S(1)}, bf16[3,288,384]{2,1,0:T(8,128)(2,1)S(1)}, u32[]{:S(2)}, u32[]{:S(2)}) %collective-permute-start.37) | collective-permute-done | bytes 663584 | tf_op jit(solution)/shard_map/ppermute | solution.py:66
  355.1 9.8 collective-permute-done.36
  366.6 4.7 collective-permute-done.39.x1
  371.3 50.8 %shard_map.219 = (bf16[3,1024,1152]{2,1,0:T(8,128)(2,1)}, bf16[3,2304,1152]{2,1,0:T(8,128)(2,1)}, bf16[3,288,768]{2,1,0:T(8,128)(2,1)}, bf16[3,288,768]{2,1,0:T(...) custom-call(s32[2]{0:T(128)} %pad_add_fusion.place_ref, ...), custom_call_target="tpu_custom_call" | custom-call | flops 32614907904 | bytes 41287680 | tf_op jit(solution)/shard_map/pallas_call | solution.py:703
  422.5 24.8 %shard_map.220 = (bf16[512,2304]{1,0:T(8,128)(2,1)}, bf16[512,2304]{1,0:T(8,128)(2,1)}, bf16[512,2304]{1,0:T(8,128)(2,1)}, bf16[512,2304]{1,0:T(8,128)(2,1)}) custom-call(bf16[3,1024,1152]{2,1,0:T(8,128)(2,1)} %get-tuple-element.239.s_ref, bf16[3,2304,1152]{2,1,0:T(8,128)(2,1)} %get-tuple-element.240.w_ref), custom_call_target="tpu_custom_call" | custom-call | flops 16307453952 | bytes 32440320 | tf_op jit(solution)/shard_map/pallas_call | solution.py:748
  447.2 6.4 collective-permute-done.40
  461.6 38.0 %collective-permute-done.45 = bf16[3,288,384]{2,1,0:T(8,128)(2,1)S(1)} collective-permute-done((bf16[3,288,384]{2,1,0:T(8,128)(2,1)S(1)}, bf16[3,288,384]{2,1,0:T(8,128)(2,1)S(1)}, u32[]{:S(2)}, u32[]{:S(2)}) %collective-permute-start.45) | collective-permute-done | bytes 663584 | tf_op jit(solution)/shard_map/ppermute | solution.py:66
  504.9 12.6 %collective-permute-done.47 = bf16[3,288,384]{2,1,0:T(8,128)(2,1)S(1)} collective-permute-done((bf16[3,288,384]{2,1,0:T(8,128)(2,1)S(1)}, bf16[3,288,384]{2,1,0:T(8,128)(2,1)S(1)}, u32[]{:S(2)}, u32[]{:S(2)}) %collective-permute-start.47) | collective-permute-done | bytes 663584 | tf_op jit(solution)/shard_map/ppermute | solution.py:66
  517.7 13.9 %collective-permute-done.48 = bf16[3,288,384]{2,1,0:T(8,128)(2,1)S(1)} collective-permute-done((bf16[3,288,384]{2,1,0:T(8,128)(2,1)S(1)}, bf16[3,288,384]{2,1,0:T(8,128)(2,1)S(1)}, u32[]{:S(2)}, u32[]{:S(2)}) %collective-permute-start.48) | collective-permute-done | bytes 663584 | tf_op jit(solution)/shard_map/ppermute | solution.py:66
  542.7 17.4 %collective-permute-done.54 = bf16[3,288,768]{2,1,0:T(8,128)(2,1)S(1)} collective-permute-done((bf16[3,288,768]{2,1,0:T(8,128)(2,1)S(1)}, bf16[3,288,768]{2,1,0:T(8,128)(2,1)S(1)}, u32[]{:S(2)}, u32[]{:S(2)}) %collective-permute-start.54) | collective-permute-done | bytes 1327136 | tf_op jit(solution)/shard_map/ppermute | solution.py:66
  576.5 8.1 shard_map.222
  584.6 17.0 %collective-permute-done.57.refs_4_ = bf16[3,288,384]{2,1,0:T(8,128)(2,1)} collective-permute-done((bf16[3,288,384]{2,1,0:T(8,128)(2,1)}, bf16[3,288,384]{2,1,0:T(8,128)(2,1)}, u32[]{:S(2)}, u32[]{:S(2)}) %collective-permute-start.57) | collective-permute-done | bytes 663584 | tf_op jit(solution)/shard_map/ppermute | solution.py:66
  601.6 17.0 %collective-permute-done.51.refs_6_ = bf16[3,288,768]{2,1,0:T(8,128)(2,1)} collective-permute-done((bf16[3,288,768]{2,1,0:T(8,128)(2,1)}, bf16[3,288,768]{2,1,0:T(8,128)(2,1)}, u32[]{:S(2)}, u32[]{:S(2)}) %collective-permute-start.51) | collective-permute-done | bytes 1327136 | tf_op jit(solution)/shard_map/ppermute | solution.py:66
  618.6 8.8 collective-permute-done.55.refs_0_
  633.0 8.5 shard_map.223
  641.5 7.4 collective-permute-done.59
  666.1 19.0 %shard_map.224 = (f32[33,288,256]{2,1,0:T(8,128)}, f32[33,288,256]{2,1,0:T(8,128)}, f32[33,3,128,128]{3,2,1,0:T(8,128)}) custom-call(s32[1]{0:T(128)} %bitcast.s_ref, bf16[3,288,768]{2,1,0:T(8,128)(2,1)} %collective-permute-done.55.refs_0_, bf16[3,288,768]{2,1,0:T(8,128)(2,1)} %get-tuple-element.289.refs_1_, ...), custom_call_target="tpu_custom_call" | custom-call | flops 3057647616 | bytes 31850496 | tf_op jit(solution)/shard_map/pallas_call | solution.py:825
  694.9 6.6 collective-permute-done.71
  705.2 15.3 %collective-permute-done.72 = f32[6,128,128]{2,1,0:T(8,128)S(1)} collective-permute-done((f32[6,128,128]{2,1,0:T(8,128)S(1)}, f32[6,128,128]{2,1,0:T(8,128)S(1)}, u32[]{:S(2)}, u32[]{:S(2)}) %collective-permute-start.72) | collective-permute-done | bytes 393248 | tf_op jit(solution)/shard_map/ppermute | solution.py:66
  730.5 6.9 collective-permute-done.73
  738.3 27.4 %collective-permute-done.74 = bf16[2,512,256]{2,1,0:T(8,128)(2,1)S(1)} collective-permute-done((bf16[2,512,256]{2,1,0:T(8,128)(2,1)S(1)}, bf16[2,512,256]{2,1,0:T(8,128)(2,1)S(1)}, u32[]{:S(2)}, u32[]{:S(2)}) %collective-permute-start.74) | collective-permute-done | bytes 524320 | tf_op jit(solution)/shard_map/ppermute | solution.py:66
  777.4 5.0 shard_map.225
  782.5 13.2 %collective-permute-done.79 = bf16[4,288,256]{2,1,0:T(8,128)(2,1)} collective-permute-done((bf16[4,288,256]{2,1,0:T(8,128)(2,1)}, bf16[4,288,256]{2,1,0:T(8,128)(2,1)}, u32[]{:S(2)}, u32[]{:S(2)}) %collective-permute-start.79) | collective-permute-done | bytes 589856 | tf_op jit(solution)/shard_map/ppermute | solution.py:66
  805.9 7.4 shard_map.226
  854.7 13.8 %collective-permute-done.94 = bf16[32,2304]{1,0:T(8,128)(2,1)} collective-permute-done((bf16[32,2304]{1,0:T(8,128)(2,1)}, bf16[32,2304]{1,0:T(8,128)(2,1)}, u32[]{:S(2)}, u32[]{:S(2)}) %collective-permute-start.94) | collective-permute-done | bytes 147488 | tf_op jit(solution)/shard_map/ppermute | solution.py:66
  875.9 5.9 collective-permute-done.95
  921.9 6.3 collective-permute-done.107
  957.3 5.8 collective-permute-done.113
  977.3 6.2 shard_map.229.refs_3_
  986.5 6.1 shard_map.230.refs_3_
  998.8 6.1 shard_map.232
  (593 shorter events, 334.6 us)
Async XLA Ops:
  4.8 36.4 %collective-permute-start.6 = (bf16[4,288,256]{2,1,0:T(8,128)(2,1)}, bf16[4,288,256]{2,1,0:T(8,128)(2,1)}, u32[]{:S(2)}, u32[]{:S(2)}) collective-permute-start(bf16[4,288,256]{2,1,0:T(8,128)(2,1)} %slice.380), channel_id=1, source_target_pairs={{0,8},{8,16},{16,24},{24,28},{28,20},{20,12},{12,4},{4,0},{1,9},{9... | collective-permute-start | bytes 1769480 | tf_op jit(solution)/shard_map/ppermute | solution.py:79
  7.8 33.8 %collective-permute-start.7 = (bf16[4,288,256]{2,1,0:T(8,128)(2,1)}, bf16[4,288,256]{2,1,0:T(8,128)(2,1)}, u32[]{:S(2)}, u32[]{:S(2)}) collective-permute-start(bf16[4,288,256]{2,1,0:T(8,128)(2,1)} %slice.380), channel_id=1, source_target_pairs={{8,0},{16,8},{24,16},{28,24},{20,28},{12,20},{4,12},{0,4},{9,1},{1... | collective-permute-start | bytes 1769480 | tf_op jit(solution)/shard_map/ppermute | solution.py:79
  13.8 72.2 %collective-permute-start.2 = (bf16[3,288,768]{2,1,0:T(8,128)(2,1)}, bf16[3,288,768]{2,1,0:T(8,128)(2,1)}, u32[]{:S(2)}, u32[]{:S(2)}) collective-permute-start(bf16[3,288,768]{2,1,0:T(8,128)(2,1)} %get-tuple-element.200.refs_0_), channel_id=1, source_target_pairs={{0,8},{4,12},{8,0},{12,4},{16,24},{20,28},{24,16},{28,20},{1,9},{5... | collective-permute-start | bytes 3981320 | tf_op jit(solution)/shard_map/ppermute | solution.py:66
  15.8 70.2 %collective-permute-start.3 = (bf16[3,288,768]{2,1,0:T(8,128)(2,1)}, bf16[3,288,768]{2,1,0:T(8,128)(2,1)}, u32[]{:S(2)}, u32[]{:S(2)}) collective-permute-start(bf16[3,288,768]{2,1,0:T(8,128)(2,1)} %get-tuple-element.200.refs_0_), channel_id=1, source_target_pairs={{0,4},{4,0},{8,12},{12,8},{16,20},{20,16},{24,28},{28,24},{1,5},{5... | collective-permute-start | bytes 3981320 | tf_op jit(solution)/shard_map/ppermute | solution.py:66
  45.3 35.5 %collective-permute-start.5 = (bf16[256,2432]{1,0:T(8,128)(2,1)S(1)}, bf16[256,2432]{1,0:T(8,128)(2,1)S(1)}, u32[]{:S(2)}, u32[]{:S(2)}) collective-permute-start(bf16[256,2432]{1,0:T(8,128)(2,1)S(1)} %pad_maximum_fusion.4), channel_id=1, source_target_pairs={{0,1},{1,0},{2,3},{3,2},{4,5},{5,4},{6,7},{7,6},{8,9},{9,8},{10,11... | collective-permute-start | bytes 3735560 | tf_op jit(solution)/shard_map/ppermute | solution.py:79
  97.2 31.8 %collective-permute-start.18 = (bf16[1616,256]{1,0:T(8,128)(2,1)}, bf16[1616,256]{1,0:T(8,128)(2,1)}, u32[]{:S(2)}, u32[]{:S(2)}) collective-permute-start(bf16[1616,256]{1,0:T(8,128)(2,1)} %fusion.35), channel_id=1, source_target_pairs={{8,0},{16,8},{24,16},{28,24},{20,28},{12,20},{4,12},{0,4},{9,1},{1... | collective-permute-start | bytes 2482184 | tf_op jit(solution)/shard_map/ppermute | solution.py:79
  97.9 108.6 %collective-permute-start.16 = (bf16[3,288,384]{2,1,0:T(8,128)(2,1)}, bf16[3,288,384]{2,1,0:T(8,128)(2,1)}, u32[]{:S(2)}, u32[]{:S(2)}) collective-permute-start(bf16[3,288,384]{2,1,0:T(8,128)(2,1)} %get-tuple-element.199.refs_8_), channel_id=1, source_target_pairs={{0,8},{4,12},{8,0},{12,4},{16,24},{20,28},{24,16},{28,20},{1,9},{5... | collective-permute-start | bytes 1990664 | tf_op jit(solution)/shard_map/ppermute | solution.py:66
  100.9 105.5 %collective-permute-start.15 = (bf16[3,288,768]{2,1,0:T(8,128)(2,1)}, bf16[3,288,768]{2,1,0:T(8,128)(2,1)S(1)}, u32[]{:S(2)}, u32[]{:S(2)}) collective-permute-start(bf16[3,288,768]{2,1,0:T(8,128)(2,1)} %collective-permute-done.2.refs_2_), channel_id=1, source_target_pairs={{0,4},{4,0},{8,12},{12,8},{16,20},{20,16},{24,28},{28,24},{1,5},{5... | collective-permute-start | bytes 3981320 | tf_op jit(solution)/shard_map/ppermute | solution.py:66
  102.2 104.3 %collective-permute-start.14 = (bf16[128,2304]{1,0:T(8,128)(2,1)S(1)}, bf16[128,2304]{1,0:T(8,128)(2,1)S(1)}, u32[]{:S(2)}, u32[]{:S(2)}) collective-permute-start(bf16[128,2304]{1,0:T(8,128)(2,1)S(1)} %copy-done.10), channel_id=1, source_target_pairs={{0,16},{4,20},{8,24},{12,28},{16,0},{20,4},{24,8},{28,12},{1,17},{... | collective-permute-start | bytes 1769480 | tf_op jit(solution)/shard_map/ppermute | solution.py:66
  117.5 43.3 %collective-permute-start.19 = (bf16[1616,256]{1,0:T(8,128)(2,1)}, bf16[1616,256]{1,0:T(8,128)(2,1)S(1)}, u32[]{:S(2)}, u32[]{:S(2)}) collective-permute-start(bf16[1616,256]{1,0:T(8,128)(2,1)} %collective-permute-done.17), channel_id=1, source_target_pairs={{0,8},{8,16},{16,24},{24,28},{28,20},{20,12},{12,4},{4,0},{1,9},{9... | collective-permute-start | bytes 2482184 | tf_op jit(solution)/shard_map/ppermute | solution.py:79
  129.0 31.9 %collective-permute-start.20 = (bf16[1616,256]{1,0:T(8,128)(2,1)}, bf16[1616,256]{1,0:T(8,128)(2,1)S(1)}, u32[]{:S(2)}, u32[]{:S(2)}) collective-permute-start(bf16[1616,256]{1,0:T(8,128)(2,1)} %collective-permute-done.18), channel_id=1, source_target_pairs={{8,0},{16,8},{24,16},{28,24},{20,28},{12,20},{4,12},{0,4},{9,1},{1... | collective-permute-start | bytes 2482184 | tf_op jit(solution)/shard_map/ppermute | solution.py:79
  190.2 32.3 %collective-permute-start.1 = (bf16[3,288,384]{2,1,0:T(8,128)(2,1)}, bf16[3,288,384]{2,1,0:T(8,128)(2,1)}, u32[]{:S(2)}, u32[]{:S(2)}) collective-permute-start(bf16[3,288,384]{2,1,0:T(8,128)(2,1)} %get-tuple-element.199.refs_8_), channel_id=1, source_target_pairs={{0,4},{4,0},{8,12},{12,8},{16,20},{20,16},{24,28},{28,24},{1,5},{5... | collective-permute-start | bytes 1990664 | tf_op jit(solution)/shard_map/ppermute | solution.py:66
  191.6 53.5 %collective-permute-start = (bf16[3,288,768]{2,1,0:T(8,128)(2,1)}, bf16[3,288,768]{2,1,0:T(8,128)(2,1)}, u32[]{:S(2)}, u32[]{:S(2)}) collective-permute-start(bf16[3,288,768]{2,1,0:T(8,128)(2,1)} %get-tuple-element.198), channel_id=1, source_target_pairs={{0,16},{4,20},{8,24},{12,28},{16,0},{20,4},{24,8},{28,12},{1,17},{... | collective-permute-start | bytes 3981320 | tf_op jit(solution)/shard_map/ppermute | solution.py:66
  208.2 37.0 %collective-permute-start.26 = (bf16[256,2304]{1,0:T(8,128)(2,1)}, bf16[256,2304]{1,0:T(8,128)(2,1)}, u32[]{:S(2)}, u32[]{:S(2)}) collective-permute-start(bf16[256,2304]{1,0:T(8,128)(2,1)} %pad_maximum_fusion.5), channel_id=1, source_target_pairs={{0,2},{1,3},{2,0},{3,1},{4,6},{5,7},{6,4},{7,5},{8,10},{9,11},{10,... | collective-permute-start | bytes 3538952 | tf_op jit(solution)/shard_map/ppermute | solution.py:66
  210.1 35.1 %collective-permute-start.25 = (bf16[3,288,384]{2,1,0:T(8,128)(2,1)}, bf16[3,288,384]{2,1,0:T(8,128)(2,1)}, u32[]{:S(2)}, u32[]{:S(2)}) collective-permute-start(bf16[3,288,384]{2,1,0:T(8,128)(2,1)} %collective-permute-done.16.refs_10_), channel_id=1, source_target_pairs={{0,4},{4,0},{8,12},{12,8},{16,20},{20,16},{24,28},{28,24},{1,5},{5... | collective-permute-start | bytes 1990664 | tf_op jit(solution)/shard_map/ppermute | solution.py:66
  245.2 31.1 %collective-permute-start.31 = (bf16[3,288,384]{2,1,0:T(8,128)(2,1)}, bf16[3,288,384]{2,1,0:T(8,128)(2,1)S(1)}, u32[]{:S(2)}, u32[]{:S(2)}) collective-permute-start(bf16[3,288,384]{2,1,0:T(8,128)(2,1)} %get-tuple-element.219), channel_id=1, source_target_pairs={{0,16},{4,20},{8,24},{12,28},{16,0},{20,4},{24,8},{28,12},{1,17},{... | collective-permute-start | bytes 1990664 | tf_op jit(solution)/shard_map/ppermute | solution.py:66
  245.3 46.0 %collective-permute-start.29 = (bf16[3,288,768]{2,1,0:T(8,128)(2,1)}, bf16[3,288,768]{2,1,0:T(8,128)(2,1)S(1)}, u32[]{:S(2)}, u32[]{:S(2)}) collective-permute-start(bf16[3,288,768]{2,1,0:T(8,128)(2,1)} %collective-permute-done.refs_4_), channel_id=1, source_target_pairs={{0,8},{4,12},{8,0},{12,4},{16,24},{20,28},{24,16},{28,20},{1,9},{5... | collective-permute-start | bytes 3981320 | tf_op jit(solution)/shard_map/ppermute | solution.py:66
  246.9 44.4 %collective-permute-start.30 = (bf16[3,288,768]{2,1,0:T(8,128)(2,1)}, bf16[3,288,768]{2,1,0:T(8,128)(2,1)S(1)}, u32[]{:S(2)}, u32[]{:S(2)}) collective-permute-start(bf16[3,288,768]{2,1,0:T(8,128)(2,1)} %collective-permute-done.refs_4_), channel_id=1, source_target_pairs={{0,4},{4,0},{8,12},{12,8},{16,20},{20,16},{24,28},{28,24},{1,5},{5... | collective-permute-start | bytes 3981320 | tf_op jit(solution)/shard_map/ppermute | solution.py:66
  249.8 41.5 %collective-permute-start.28 = (bf16[128,2304]{1,0:T(8,128)(2,1)S(1)}, bf16[128,2304]{1,0:T(8,128)(2,1)S(1)}, u32[]{:S(2)}, u32[]{:S(2)}) collective-permute-start(bf16[128,2304]{1,0:T(8,128)(2,1)S(1)} %slice.467), channel_id=1, source_target_pairs={{0,2},{1,3},{2,0},{3,1},{4,6},{5,7},{6,4},{7,5},{8,10},{9,11},{10,... | collective-permute-start | bytes 1769480 | tf_op jit(solution)/shard_map/ppermute | solution.py:66
  291.3 30.8 %collective-permute-start.34 = (bf16[3,288,384]{2,1,0:T(8,128)(2,1)S(1)}, bf16[3,288,384]{2,1,0:T(8,128)(2,1)S(1)}, u32[]{:S(2)}, u32[]{:S(2)}) collective-permute-start(bf16[3,288,384]{2,1,0:T(8,128)(2,1)S(1)} %collective-permute-done.31.refs_12_), channel_id=1, source_target_pairs={{0,8},{4,12},{8,0},{12,4},{16,24},{20,28},{24,16},{28,20},{1,9},{5... | collective-permute-start | bytes 1990664 | tf_op jit(solution)/shard_map/ppermute | solution.py:66
  291.6 30.5 %collective-permute-start.35 = (bf16[3,288,384]{2,1,0:T(8,128)(2,1)S(1)}, bf16[3,288,384]{2,1,0:T(8,128)(2,1)S(1)}, u32[]{:S(2)}, u32[]{:S(2)}) collective-permute-start(bf16[3,288,384]{2,1,0:T(8,128)(2,1)S(1)} %collective-permute-done.31.refs_12_), channel_id=1, source_target_pairs={{0,4},{4,0},{8,12},{12,8},{16,20},{20,16},{24,28},{28,24},{1,5},{5... | collective-permute-start | bytes 1990664 | tf_op jit(solution)/shard_map/ppermute | solution.py:66
  291.9 44.5 %collective-permute-start.33 = (bf16[3,288,768]{2,1,0:T(8,128)(2,1)S(1)}, bf16[3,288,768]{2,1,0:T(8,128)(2,1)S(1)}, u32[]{:S(2)}, u32[]{:S(2)}) collective-permute-start(bf16[3,288,768]{2,1,0:T(8,128)(2,1)S(1)} %collective-permute-done.29.refs_6_), channel_id=1, source_target_pairs={{0,4},{4,0},{8,12},{12,8},{16,20},{20,16},{24,28},{28,24},{1,5},{5... | collective-permute-start | bytes 3981320 | tf_op jit(solution)/shard_map/ppermute | solution.py:66
  336.4 28.6 %collective-permute-start.38 = (bf16[512,2304]{1,0:T(8,128)(2,1)S(1)}, bf16[512,2304]{1,0:T(8,128)(2,1)}, u32[]{:S(2)}, u32[]{:S(2)}) collective-permute-start(bf16[512,2304]{1,0:T(8,128)(2,1)S(1)} %constant_dynamic-update-slice_fusion.y0), channel_id=1, source_target_pairs={{0,1},{1,0},{2,3},{3,2},{4,5},{5,4},{6,7},{7,6},{8,9},{9,8},{10,11... | collective-permute-start | bytes 7077896 | tf_op jit(solution)/shard_map/ppermute | solution.py:66
  336.6 28.4 %collective-permute-start.36 = (bf16[256,2304]{1,0:T(8,128)(2,1)S(1)}, bf16[256,2304]{1,0:T(8,128)(2,1)S(1)}, u32[]{:S(2)}, u32[]{:S(2)}) collective-permute-start(bf16[256,2304]{1,0:T(8,128)(2,1)S(1)} %pad_maximum_fusion.6), channel_id=1, source_target_pairs={{0,2},{1,3},{2,0},{3,1},{4,6},{5,7},{6,4},{7,5},{8,10},{9,11},{10,... | collective-permute-start | bytes 3538952 | tf_op jit(solution)/shard_map/ppermute | solution.py:66
  422.1 31.5 %collective-permute-start.40 = (bf16[3,288,768]{2,1,0:T(8,128)(2,1)}, bf16[3,288,768]{2,1,0:T(8,128)(2,1)}, u32[]{:S(2)}, u32[]{:S(2)}) collective-permute-start(bf16[3,288,768]{2,1,0:T(8,128)(2,1)} %get-tuple-element.238), channel_id=1, source_target_pairs={{0,4},{4,0},{8,12},{12,8},{16,20},{20,16},{24,28},{28,24},{1,5},{5... | collective-permute-start | bytes 3981320 | tf_op jit(solution)/shard_map/ppermute | solution.py:66
  453.7 46.3 %collective-permute-start.44 = (bf16[3,288,768]{2,1,0:T(8,128)(2,1)}, bf16[3,288,768]{2,1,0:T(8,128)(2,1)S(1)}, u32[]{:S(2)}, u32[]{:S(2)}) collective-permute-start(bf16[3,288,768]{2,1,0:T(8,128)(2,1)} %get-tuple-element.250), channel_id=1, source_target_pairs={{0,4},{4,0},{8,12},{12,8},{16,20},{20,16},{24,28},{28,24},{1,5},{5... | collective-permute-start | bytes 3981320 | tf_op jit(solution)/shard_map/ppermute | solution.py:66
  456.0 45.7 %collective-permute-start.43 = (bf16[3,288,768]{2,1,0:T(8,128)(2,1)S(1)}, bf16[3,288,768]{2,1,0:T(8,128)(2,1)S(1)}, u32[]{:S(2)}, u32[]{:S(2)}) collective-permute-start(bf16[3,288,768]{2,1,0:T(8,128)(2,1)S(1)} %add_convert_fusion.2), channel_id=1, source_target_pairs={{0,8},{4,12},{8,0},{12,4},{16,24},{20,28},{24,16},{28,20},{1,9},{5... | collective-permute-start | bytes 3981320 | tf_op jit(solution)/shard_map/ppermute | solution.py:66
  459.1 42.6 %collective-permute-start.42 = (bf16[256,2304]{1,0:T(8,128)(2,1)S(1)}, bf16[256,2304]{1,0:T(8,128)(2,1)S(1)}, u32[]{:S(2)}, u32[]{:S(2)}) collective-permute-start(bf16[256,2304]{1,0:T(8,128)(2,1)S(1)} %slice.464), channel_id=1, source_target_pairs={{0,2},{1,3},{2,0},{3,1},{4,6},{5,7},{6,4},{7,5},{8,10},{9,11},{10,... | collective-permute-start | bytes 3538952 | tf_op jit(solution)/shard_map/ppermute | solution.py:66
  460.6 39.0 %collective-permute-start.45 = (bf16[3,288,384]{2,1,0:T(8,128)(2,1)S(1)}, bf16[3,288,384]{2,1,0:T(8,128)(2,1)S(1)}, u32[]{:S(2)}, u32[]{:S(2)}) collective-permute-start(bf16[3,288,384]{2,1,0:T(8,128)(2,1)S(1)} %copy-done.73), channel_id=1, source_target_pairs={{0,4},{4,0},{8,12},{12,8},{16,20},{20,16},{24,28},{28,24},{1,5},{5... | collective-permute-start | bytes 1990664 | tf_op jit(solution)/shard_map/ppermute | solution.py:66
  461.6 70.1 %collective-permute-start.50 = (bf16[512,2304]{1,0:T(8,128)(2,1)S(1)}, bf16[512,2304]{1,0:T(8,128)(2,1)S(1)}, u32[]{:S(2)}, u32[]{:S(2)}) collective-permute-start(bf16[512,2304]{1,0:T(8,128)(2,1)S(1)} %copy-done.62), channel_id=1, source_target_pairs={{0,1},{1,0},{2,3},{3,2},{4,5},{5,4},{6,7},{7,6},{8,9},{9,8},{10,11... | collective-permute-start | bytes 7077896 | tf_op jit(solution)/shard_map/ppermute | solution.py:66
  499.9 31.7 %collective-permute-start.48 = (bf16[3,288,384]{2,1,0:T(8,128)(2,1)S(1)}, bf16[3,288,384]{2,1,0:T(8,128)(2,1)S(1)}, u32[]{:S(2)}, u32[]{:S(2)}) collective-permute-start(bf16[3,288,384]{2,1,0:T(8,128)(2,1)S(1)} %copy-done.69), channel_id=1, source_target_pairs={{0,4},{4,0},{8,12},{12,8},{16,20},{20,16},{24,28},{28,24},{1,5},{5... | collective-permute-start | bytes 1990664 | tf_op jit(solution)/shard_map/ppermute | solution.py:66
  501.9 29.8 %collective-permute-start.49 = (bf16[3,288,384]{2,1,0:T(8,128)(2,1)S(1)}, bf16[3,288,384]{2,1,0:T(8,128)(2,1)S(1)}, u32[]{:S(2)}, u32[]{:S(2)}) collective-permute-start(bf16[3,288,384]{2,1,0:T(8,128)(2,1)S(1)} %add_convert_fusion.5), channel_id=1, source_target_pairs={{0,8},{4,12},{8,0},{12,4},{16,24},{20,28},{24,16},{28,20},{1,9},{5... | collective-permute-start | bytes 1990664 | tf_op jit(solution)/shard_map/ppermute | solution.py:66
  517.5 42.7 %collective-permute-start.54 = (bf16[3,288,768]{2,1,0:T(8,128)(2,1)S(1)}, bf16[3,288,768]{2,1,0:T(8,128)(2,1)S(1)}, u32[]{:S(2)}, u32[]{:S(2)}) collective-permute-start(bf16[3,288,768]{2,1,0:T(8,128)(2,1)S(1)} %copy-done.64), channel_id=1, source_target_pairs={{0,4},{4,0},{8,12},{12,8},{16,20},{20,16},{24,28},{28,24},{1,5},{5... | collective-permute-start | bytes 3981320 | tf_op jit(solution)/shard_map/ppermute | solution.py:66
  532.0 30.4 %collective-permute-start.53 = (bf16[3,288,384]{2,1,0:T(8,128)(2,1)S(1)}, bf16[3,288,384]{2,1,0:T(8,128)(2,1)S(1)}, u32[]{:S(2)}, u32[]{:S(2)}) collective-permute-start(bf16[3,288,384]{2,1,0:T(8,128)(2,1)S(1)} %add_convert_fusion.4), channel_id=1, source_target_pairs={{0,16},{4,20},{8,24},{12,28},{16,0},{20,4},{24,8},{28,12},{1,17},{... | collective-permute-start | bytes 1990664 | tf_op jit(solution)/shard_map/ppermute | solution.py:66
  539.1 62.5 %collective-permute-start.56 = (bf16[3,288,768]{2,1,0:T(8,128)(2,1)}, bf16[3,288,768]{2,1,0:T(8,128)(2,1)}, u32[]{:S(2)}, u32[]{:S(2)}) collective-permute-start(bf16[3,288,768]{2,1,0:T(8,128)(2,1)} %get-tuple-element.269), channel_id=1, source_target_pairs={{0,4},{4,0},{8,12},{12,8},{16,20},{20,16},{24,28},{28,24},{1,5},{5... | collective-permute-start | bytes 3981320 | tf_op jit(solution)/shard_map/ppermute | solution.py:66
  539.4 62.2 %collective-permute-start.57 = (bf16[3,288,384]{2,1,0:T(8,128)(2,1)}, bf16[3,288,384]{2,1,0:T(8,128)(2,1)}, u32[]{:S(2)}, u32[]{:S(2)}) collective-permute-start(bf16[3,288,384]{2,1,0:T(8,128)(2,1)} %get-tuple-element.270), channel_id=1, source_target_pairs={{0,4},{4,0},{8,12},{12,8},{16,20},{20,16},{24,28},{28,24},{1,5},{5... | collective-permute-start | bytes 1990664 | tf_op jit(solution)/shard_map/ppermute | solution.py:66
  560.1 58.5 %collective-permute-start.51 = (bf16[3,288,768]{2,1,0:T(8,128)(2,1)}, bf16[3,288,768]{2,1,0:T(8,128)(2,1)}, u32[]{:S(2)}, u32[]{:S(2)}) collective-permute-start(bf16[3,288,768]{2,1,0:T(8,128)(2,1)} %add_convert_fusion.1), channel_id=1, source_target_pairs={{0,16},{4,20},{8,24},{12,28},{16,0},{20,4},{24,8},{28,12},{1,17},{... | collective-permute-start | bytes 3981320 | tf_op jit(solution)/shard_map/ppermute | solution.py:66
  568.1 59.3 %collective-permute-start.55 = (bf16[3,288,768]{2,1,0:T(8,128)(2,1)}, bf16[3,288,768]{2,1,0:T(8,128)(2,1)}, u32[]{:S(2)}, u32[]{:S(2)}) collective-permute-start(bf16[3,288,768]{2,1,0:T(8,128)(2,1)} %add_convert_fusion), channel_id=1, source_target_pairs={{0,8},{4,12},{8,0},{12,4},{16,24},{20,28},{24,16},{28,20},{1,9},{5... | collective-permute-start | bytes 3981320 | tf_op jit(solution)/shard_map/ppermute | solution.py:66
  687.8 34.4 %collective-permute-start.70 = (bf16[4,288,256]{2,1,0:T(8,128)(2,1)S(1)}, bf16[4,288,256]{2,1,0:T(8,128)(2,1)S(1)}, u32[]{:S(2)}, u32[]{:S(2)}) collective-permute-start(bf16[4,288,256]{2,1,0:T(8,128)(2,1)S(1)} %pad_maximum_fusion.14), channel_id=1, source_target_pairs={{8,0},{16,8},{24,16},{28,24},{20,28},{12,20},{4,12},{0,4},{9,1},{1... | collective-permute-start | bytes 1769480 | tf_op jit(solution)/shard_map/ppermute | solution.py:66
  691.2 31.0 %collective-permute-start.69 = (bf16[4,288,256]{2,1,0:T(8,128)(2,1)S(1)}, bf16[4,288,256]{2,1,0:T(8,128)(2,1)S(1)}, u32[]{:S(2)}, u32[]{:S(2)}) collective-permute-start(bf16[4,288,256]{2,1,0:T(8,128)(2,1)S(1)} %pad_maximum_fusion.13), channel_id=1, source_target_pairs={{0,8},{8,16},{16,24},{24,28},{28,20},{20,12},{12,4},{4,0},{1,9},{9... | collective-permute-start | bytes 1769480 | tf_op jit(solution)/shard_map/ppermute | solution.py:66
  692.7 29.4 %collective-permute-start.67 = (bf16[2,512,256]{2,1,0:T(8,128)(2,1)S(1)}, bf16[2,512,256]{2,1,0:T(8,128)(2,1)S(1)}, u32[]{:S(2)}, u32[]{:S(2)}) collective-permute-start(bf16[2,512,256]{2,1,0:T(8,128)(2,1)S(1)} %get-tuple-element.428), channel_id=1, source_target_pairs={{0,8},{8,16},{16,24},{24,28},{28,20},{20,12},{12,4},{4,0},{1,9},{9... | collective-permute-start | bytes 1572872 | tf_op jit(solution)/shard_map/ppermute | solution.py:66
  693.1 29.0 %collective-permute-start.68 = (bf16[2,512,256]{2,1,0:T(8,128)(2,1)S(1)}, bf16[2,512,256]{2,1,0:T(8,128)(2,1)S(1)}, u32[]{:S(2)}, u32[]{:S(2)}) collective-permute-start(bf16[2,512,256]{2,1,0:T(8,128)(2,1)S(1)} %get-tuple-element.427), channel_id=1, source_target_pairs={{8,0},{16,8},{24,16},{28,24},{20,28},{12,20},{4,12},{0,4},{9,1},{1... | collective-permute-start | bytes 1572872 | tf_op jit(solution)/shard_map/ppermute | solution.py:66
  725.9 41.7 %collective-permute-start.78 = (f32[12,128,128]{2,1,0:T(8,128)S(1)}, f32[12,128,128]{2,1,0:T(8,128)S(1)}, u32[]{:S(2)}, u32[]{:S(2)}) collective-permute-start(f32[12,128,128]{2,1,0:T(8,128)S(1)} %pad_maximum_fusion.11), channel_id=1, source_target_pairs={{8,0},{16,8},{24,16},{28,24},{20,28},{12,20},{4,12},{0,4},{9,1},{1... | collective-permute-start | bytes 2359304 | tf_op jit(solution)/shard_map/ppermute | solution.py:66
  726.3 41.3 %collective-permute-start.77 = (f32[12,128,128]{2,1,0:T(8,128)S(1)}, f32[12,128,128]{2,1,0:T(8,128)S(1)}, u32[]{:S(2)}, u32[]{:S(2)}) collective-permute-start(f32[12,128,128]{2,1,0:T(8,128)S(1)} %pad_maximum_fusion.10), channel_id=1, source_target_pairs={{0,8},{8,16},{16,24},{24,28},{28,20},{20,12},{12,4},{4,0},{1,9},{9... | collective-permute-start | bytes 2359304 | tf_op jit(solution)/shard_map/ppermute | solution.py:66
  728.4 39.1 %collective-permute-start.75 = (bf16[4,288,256]{2,1,0:T(8,128)(2,1)S(1)}, bf16[4,288,256]{2,1,0:T(8,128)(2,1)S(1)}, u32[]{:S(2)}, u32[]{:S(2)}) collective-permute-start(bf16[4,288,256]{2,1,0:T(8,128)(2,1)S(1)} %get-tuple-element.418), channel_id=1, source_target_pairs={{0,8},{8,16},{16,24},{24,28},{28,20},{20,12},{12,4},{4,0},{1,9},{9... | collective-permute-start | bytes 1769480 | tf_op jit(solution)/shard_map/ppermute | solution.py:66
  728.5 39.0 %collective-permute-start.76 = (bf16[4,288,256]{2,1,0:T(8,128)(2,1)S(1)}, bf16[4,288,256]{2,1,0:T(8,128)(2,1)S(1)}, u32[]{:S(2)}, u32[]{:S(2)}) collective-permute-start(bf16[4,288,256]{2,1,0:T(8,128)(2,1)S(1)} %get-tuple-element.417), channel_id=1, source_target_pairs={{8,0},{16,8},{24,16},{28,24},{20,28},{12,20},{4,12},{0,4},{9,1},{1... | collective-permute-start | bytes 1769480 | tf_op jit(solution)/shard_map/ppermute | solution.py:66
  737.4 28.3 %collective-permute-start.74 = (bf16[2,512,256]{2,1,0:T(8,128)(2,1)S(1)}, bf16[2,512,256]{2,1,0:T(8,128)(2,1)S(1)}, u32[]{:S(2)}, u32[]{:S(2)}) collective-permute-start(bf16[2,512,256]{2,1,0:T(8,128)(2,1)S(1)} %get-tuple-element.425), channel_id=1, source_target_pairs={{8,0},{16,8},{24,16},{28,24},{20,28},{12,20},{4,12},{0,4},{9,1},{1... | collective-permute-start | bytes 1572872 | tf_op jit(solution)/shard_map/ppermute | solution.py:66
  770.3 28.4 %collective-permute-start.81 = (f32[12,128,128]{2,1,0:T(8,128)}, f32[12,128,128]{2,1,0:T(8,128)}, u32[]{:S(2)}, u32[]{:S(2)}) collective-permute-start(f32[12,128,128]{2,1,0:T(8,128)} %get-tuple-element.408), channel_id=1, source_target_pairs={{0,8},{8,16},{16,24},{24,28},{28,20},{20,12},{12,4},{4,0},{1,9},{9... | collective-permute-start | bytes 2359304 | tf_op jit(solution)/shard_map/ppermute | solution.py:66
  (155 other events, 2154.7 us)
where the time goes:
time: 1010 us
  waiting for transfers between devices  517 us (51%)
  Pallas kernels  183 us (18%)
  starting transfers between devices  140 us (14%)
  other arithmetic  74.9 us (7%)
  local copies, waits for them, and re-layouts  52.7 us (5%)
  matrix products  18.8 us (2%)
  between operations  18.6 us (2%)
    ppermute x104, waiting for transfers between devices, stage(): arrived = [[lax.ppermute(*send) for send in flow.sends] for flow in flows]  408 us
    ppermute x104, starting transfers between devices, stage(): arrived = [[lax.ppermute(*send) for send in flow.sends] for flow in flows]  121 us
    ppermute x18, waiting for transfers between devices, run(): flow.advance([lax.ppermute(*send) for send in flow.sends])  107 us
    pallas_call x1, Pallas kernels, ffn_front(): pl.pallas_call(body, grid_spec=pltpu.PrefetchScalarGridSpec(num_scalar_pr...  50.8 us
    pallas_call x1, Pallas kernels, ffn_back(): pl.pallas_call(body, grid=(d // wide,), in_specs=[pl.BlockSpec((3, t, u),...  24.8 us
    pallas_call x4, Pallas kernels, renew(): pl.pallas_call(body, grid_spec=pltpu.PrefetchScalarGridSpec(num_scalar_pr...  22.4 us
  transfers between devices with their start and end apart: 125, of which 56 were waited for; matrix products, arithmetic and copies ran while one was open for 11% of the time, Pallas kernels for 12%

commit v1 on v0

--- a/solution.py
+++ b/solution.py
@@ -1077,7 +1077,7 @@
     pieces = len(ffn_grads) // 2
     reduce = [Reduce(taker(ffn_grads[:pieces])), Reduce(taker(ffn_grads[pieces:]))]
     *down_part, dx_kept, dx_sent = stage([reduce[0].y(2)], ffn_back(ffn_sides, ffn_full))
-    out_flow = Flow(scatter_rows(*down_part, WIDE_MOVES, 4))
+    out_flow = Flow(scatter_rows(*down_part, WIDE_MOVES, 2))
     dx_flow = Flow(scatter_rows(dx_kept, dx_sent, WIDE_MOVES))
     dx_flow.advance([lax.ppermute(*send) for send in dx_flow.sends])
     stage([dx_flow, reduce[0].near(2), reduce[0].y(3), reduce[1].y(2)])
@@ -1122,13 +1122,13 @@
 
     key_flow = Flow(ring.scatter(ring.part(grad_keys_values, 0), key_heads))
     (outer,) = stage(
-        [key_flow, late_near, out_flow],
+        [key_flow, late_near],
         [block_outer([group_in, group_grad], [grad_queries, mixed_heads], model_width)],
     )
     (own_early, other_early), (own_late, other_late) = (part.value() for part in reduce)
     first_flow = weight_sums(outer)
     weight_grads, new_momentum, grams = stage(
-        [key_flow, first_flow],
+        [key_flow, first_flow, out_flow],
         ffn_moment(
             jnp.reshape(parity, (1,)),
             [own_early, own_late],
@@ -1147,7 +1147,7 @@
     grad_keys = (key_value_sums[:key_heads] * scale).astype(BF16)
     grad_values = key_value_sums[key_heads:].astype(BF16)
     grad_keys_values = jnp.concatenate([grad_keys, grad_values], axis=0)
-    (outer,) = stage([first_flow, gram_flow, out_flow], [block_outer([group_in], [grad_keys_values], model_width)])
+    (outer,) = stage([first_flow, gram_flow], [block_outer([group_in], [grad_keys_values], model_width)])
     finish(first_flow)
     second_flow = weight_sums(outer)
     pairs = [k for k in range(gate_mark // 2) if not query_heads <= 2 * k < out_mark]
@@ -1163,9 +1163,8 @@
     finish(gram_flow)
     gram_value = gram_flow.value
     while second_flow.sends is not None:
-        (gram_value,) = stage([second_flow, last_flow, out_flow], [gram_value])
-    finish(last_flow, out_flow)
-    block_out = (residual + out_flow.value).astype(BF16)
+        (gram_value,) = stage([second_flow, last_flow], [gram_value], idle=[out_flow])
+    finish(last_flow)
     grad_input_norm, grad_gain_one = norm_one_back(last_flow.value)
     grad_input = grad_residual + grad_input_norm
     gain_flow = Flow(total_sum(jnp.stack([grad_gain_one, grad_gain_two])))
@@ -1178,11 +1177,13 @@
     late_grams = jnp.pad(late_grams, ((0, late_cap * data_count - late_count), (0, 0), (0, 0), (0, 0)))
     late_gram_flow = Flow(gram_sums(ring, late_grams, late_cap))
     (gram_value,) = stage([late_gram_flow, gain_flow], [gram_value])
-    (factors,) = stage([late_gram_flow, gain_flow], [newton_factor(gram_value, growth)])
+    (factors,) = stage([late_gram_flow, gain_flow, out_flow], [newton_factor(gram_value, growth)])
     factor_flow = Flow(all_factors(ring, factors))
     while late_gram_flow.sends is not None:
         stage([late_gram_flow, factor_flow, gain_flow])
-    (late_factors,) = stage([factor_flow, gain_flow], [newton_factor(late_gram_flow.value, growth)])
+    (late_factors,) = stage([factor_flow, gain_flow, out_flow], [newton_factor(late_gram_flow.value, growth)])
+    finish(out_flow)
+    block_out = (residual + out_flow.value).astype(BF16)
     late_factor_flow = Flow(all_factors(ring, late_factors))
     while factor_flow.sends is not None:
         stage([factor_flow, late_factor_flow, gain_flow])

time: 1010 us -> 1000 us (0.990)
  waiting for transfers between devices: 517 us -> 492 us
    ppermute x104 -> x102, waiting for transfers between devices: 408 us -> 383 us  [stage(): arrived = [[lax.ppermute(*send) for send in flow.sends] for flow in flows]]
    ppermute x104 -> x102, starting transfers between devices: 121 us -> 125 us  [stage(): arrived = [[lax.ppermute(*send) for send in flow.sends] for flow in flows]]
  transfers between devices with their start and end apart: 125 -> 123, of which waited for: 56 -> 54; matrix products, arithmetic and copies ran while one was open for 11% -> 12% of each run, Pallas kernels for 12% -> 12%
where the time goes in v1:
time: 1000 us; the launch traced here: 992 us
  waiting for transfers between devices  492 us (49%)
  Pallas kernels  183 us (18%)
  starting transfers between devices  144 us (14%)
  other arithmetic  80.4 us (8%)
  local copies, waits for them, and re-layouts  55 us (6%)
  matrix products  18.8 us (2%)
  between operations  18.6 us (2%)
    ppermute x102, waiting for transfers between devices, stage(): arrived = [[lax.ppermute(*send) for send in flow.sends] for flow in flows]  383 us
    ppermute x102, starting transfers between devices, stage(): arrived = [[lax.ppermute(*send) for send in flow.sends] for flow in flows]  125 us
    ppermute x18, waiting for transfers between devices, run(): flow.advance([lax.ppermute(*send) for send in flow.sends])  108 us
    pallas_call x1, Pallas kernels, ffn_front(): pl.pallas_call(body, grid_spec=pltpu.PrefetchScalarGridSpec(num_scalar_pr...  50.8 us
    pallas_call x1, Pallas kernels, ffn_back(): pl.pallas_call(body, grid=(d // wide,), in_specs=[pl.BlockSpec((3, t, u),...  24.6 us
    pallas_call x4, Pallas kernels, renew(): pl.pallas_call(body, grid_spec=pltpu.PrefetchScalarGridSpec(num_scalar_pr...  22.4 us
  transfers between devices with their start and end apart: 123, of which 54 were waited for; matrix products, arithmetic and copies ran while one was open for 12% of the time, Pallas kernels for 12%

profile of v1, /device:TPU:0, one launch (start us, length us, event | category | flops | bytes accessed | tf_op | source)
XLA Modules:
  0.0 992.2 jit_solution(14686021038249329825)
XLA Ops:
  7.9 6.0 shard_map.214
  45.1 17.2 %collective-permute-done.8 = bf16[4,288,256]{2,1,0:T(8,128)(2,1)S(1)} collective-permute-done((bf16[4,288,256]{2,1,0:T(8,128)(2,1)}, bf16[4,288,256]{2,1,0:T(8,128)(2,1)S(1)}, u32[]{:S(2)}, u32[]{:S(2)}) %collective-permute-start.8) | collective-permute-done | bytes 589856 | tf_op jit(solution)/shard_map/ppermute | solution.py:79
  68.1 8.8 collective-permute-done.10
  86.1 6.6 shard_map.216
  105.1 12.4 %collective-permute-done.17 = bf16[1616,256]{1,0:T(8,128)(2,1)} collective-permute-done((bf16[1616,256]{1,0:T(8,128)(2,1)}, bf16[1616,256]{1,0:T(8,128)(2,1)}, u32[]{:S(2)}, u32[]{:S(2)}) %collective-permute-start.17) | collective-permute-done | bytes 827424 | tf_op jit(solution)/shard_map/ppermute | solution.py:79
  118.9 10.1 %collective-permute-done.18 = bf16[1616,256]{1,0:T(8,128)(2,1)} collective-permute-done((bf16[1616,256]{1,0:T(8,128)(2,1)}, bf16[1616,256]{1,0:T(8,128)(2,1)}, u32[]{:S(2)}, u32[]{:S(2)}) %collective-permute-start.18) | collective-permute-done | bytes 827424 | tf_op jit(solution)/shard_map/ppermute | solution.py:79
  131.4 29.4 %collective-permute-done.19 = bf16[1616,256]{1,0:T(8,128)(2,1)S(1)} collective-permute-done((bf16[1616,256]{1,0:T(8,128)(2,1)}, bf16[1616,256]{1,0:T(8,128)(2,1)S(1)}, u32[]{:S(2)}, u32[]{:S(2)}) %collective-permute-start.19) | collective-permute-done | bytes 827424 | tf_op jit(solution)/shard_map/ppermute | solution.py:79
  163.0 16.3 %collective-permute-done.21 = bf16[1616,256]{1,0:T(8,128)(2,1)S(1)} collective-permute-done((bf16[1616,256]{1,0:T(8,128)(2,1)S(1)}, bf16[1616,256]{1,0:T(8,128)(2,1)S(1)}, u32[]{:S(2)}, u32[]{:S(2)}) %collective-permute-start.21) | collective-permute-done | bytes 827424 | tf_op jit(solution)/shard_map/ppermute | solution.py:79
  182.1 8.0 collective-permute-done.23
  192.0 13.2 %collective-permute-start = (bf16[3,288,768]{2,1,0:T(8,128)(2,1)}, bf16[3,288,768]{2,1,0:T(8,128)(2,1)}, u32[]{:S(2)}, u32[]{:S(2)}) collective-permute-start(bf16[3,288,768]{2,1,0:T(8,128)(2,1)} %get-tuple-element.199), channel_id=1, source_target_pairs={{0,16},{4,20},{8,24},{12,28},{16,0},{20,4},{24,8},{28,12},{1,17},{... | collective-permute-start | bytes 3981320 | tf_op jit(solution)/shard_map/ppermute | solution.py:66
  212.9 5.2 shard_map.217
  218.1 5.0 shard_map.218
  223.1 22.3 %collective-permute-done.refs_4_ = bf16[3,288,768]{2,1,0:T(8,128)(2,1)} collective-permute-done((bf16[3,288,768]{2,1,0:T(8,128)(2,1)}, bf16[3,288,768]{2,1,0:T(8,128)(2,1)}, u32[]{:S(2)}, u32[]{:S(2)}) %collective-permute-start) | collective-permute-done | bytes 1327136 | tf_op jit(solution)/shard_map/ppermute | solution.py:66
  253.1 23.2 %collective-permute-done.31.refs_12_ = bf16[3,288,384]{2,1,0:T(8,128)(2,1)S(1)} collective-permute-done((bf16[3,288,384]{2,1,0:T(8,128)(2,1)}, bf16[3,288,384]{2,1,0:T(8,128)(2,1)S(1)}, u32[]{:S(2)}, u32[]{:S(2)}) %collective-permute-start.31) | collective-permute-done | bytes 663584 | tf_op jit(solution)/shard_map/ppermute | solution.py:66
  276.3 15.3 %collective-permute-done.29.refs_6_ = bf16[3,288,768]{2,1,0:T(8,128)(2,1)S(1)} collective-permute-done((bf16[3,288,768]{2,1,0:T(8,128)(2,1)}, bf16[3,288,768]{2,1,0:T(8,128)(2,1)S(1)}, u32[]{:S(2)}, u32[]{:S(2)}) %collective-permute-start.29) | collective-permute-done | bytes 1327136 | tf_op jit(solution)/shard_map/ppermute | solution.py:66
  296.7 25.7 %collective-permute-done.32 = bf16[128,2304]{1,0:T(8,128)(2,1)S(1)} collective-permute-done((bf16[128,2304]{1,0:T(8,128)(2,1)S(1)}, bf16[128,2304]{1,0:T(8,128)(2,1)S(1)}, u32[]{:S(2)}, u32[]{:S(2)}) %collective-permute-start.32) | collective-permute-done | bytes 589856 | tf_op jit(solution)/shard_map/ppermute | solution.py:66
  322.4 14.3 %collective-permute-done.33.refs_7_ = bf16[3,288,768]{2,1,0:T(8,128)(2,1)S(1)} collective-permute-done((bf16[3,288,768]{2,1,0:T(8,128)(2,1)S(1)}, bf16[3,288,768]{2,1,0:T(8,128)(2,1)S(1)}, u32[]{:S(2)}, u32[]{:S(2)}) %collective-permute-start.33) | collective-permute-done | bytes 1327136 | tf_op jit(solution)/shard_map/ppermute | solution.py:66
  338.6 16.7 %collective-permute-done.37.refs_15_ = bf16[3,288,384]{2,1,0:T(8,128)(2,1)S(1)} collective-permute-done((bf16[3,288,384]{2,1,0:T(8,128)(2,1)S(1)}, bf16[3,288,384]{2,1,0:T(8,128)(2,1)S(1)}, u32[]{:S(2)}, u32[]{:S(2)}) %collective-permute-start.37) | collective-permute-done | bytes 663584 | tf_op jit(solution)/shard_map/ppermute | solution.py:66
  355.4 9.8 collective-permute-done.36
  366.9 4.7 collective-permute-done.39.x1
  371.5 50.8 %shard_map.219 = (bf16[3,1024,1152]{2,1,0:T(8,128)(2,1)}, bf16[3,2304,1152]{2,1,0:T(8,128)(2,1)}, bf16[3,288,768]{2,1,0:T(8,128)(2,1)}, bf16[3,288,768]{2,1,0:T(...) custom-call(s32[2]{0:T(128)} %pad_add_fusion.place_ref, ...), custom_call_target="tpu_custom_call" | custom-call | flops 32614907904 | bytes 41287680 | tf_op jit(solution)/shard_map/pallas_call | solution.py:703
  422.7 24.6 %shard_map.220 = (bf16[512,2304]{1,0:T(8,128)(2,1)}, bf16[512,2304]{1,0:T(8,128)(2,1)}, bf16[512,2304]{1,0:T(8,128)(2,1)}, bf16[512,2304]{1,0:T(8,128)(2,1)}) custom-call(bf16[3,1024,1152]{2,1,0:T(8,128)(2,1)} %get-tuple-element.240.s_ref, bf16[3,2304,1152]{2,1,0:T(8,128)(2,1)} %get-tuple-element.241.w_ref), custom_call_target="tpu_custom_call" | custom-call | flops 16307453952 | bytes 32440320 | tf_op jit(solution)/shard_map/pallas_call | solution.py:748
  447.3 6.6 collective-permute-done.40
  461.9 38.0 %collective-permute-done.45 = bf16[3,288,384]{2,1,0:T(8,128)(2,1)S(1)} collective-permute-done((bf16[3,288,384]{2,1,0:T(8,128)(2,1)S(1)}, bf16[3,288,384]{2,1,0:T(8,128)(2,1)S(1)}, u32[]{:S(2)}, u32[]{:S(2)}) %collective-permute-start.45) | collective-permute-done | bytes 663584 | tf_op jit(solution)/shard_map/ppermute | solution.py:66
  504.8 12.9 %collective-permute-done.47 = bf16[3,288,384]{2,1,0:T(8,128)(2,1)S(1)} collective-permute-done((bf16[3,288,384]{2,1,0:T(8,128)(2,1)S(1)}, bf16[3,288,384]{2,1,0:T(8,128)(2,1)S(1)}, u32[]{:S(2)}, u32[]{:S(2)}) %collective-permute-start.47) | collective-permute-done | bytes 663584 | tf_op jit(solution)/shard_map/ppermute | solution.py:66
  518.0 13.9 %collective-permute-done.48 = bf16[3,288,384]{2,1,0:T(8,128)(2,1)S(1)} collective-permute-done((bf16[3,288,384]{2,1,0:T(8,128)(2,1)S(1)}, bf16[3,288,384]{2,1,0:T(8,128)(2,1)S(1)}, u32[]{:S(2)}, u32[]{:S(2)}) %collective-permute-start.48) | collective-permute-done | bytes 663584 | tf_op jit(solution)/shard_map/ppermute | solution.py:66
  542.7 17.7 %collective-permute-done.54 = bf16[3,288,768]{2,1,0:T(8,128)(2,1)S(1)} collective-permute-done((bf16[3,288,768]{2,1,0:T(8,128)(2,1)S(1)}, bf16[3,288,768]{2,1,0:T(8,128)(2,1)S(1)}, u32[]{:S(2)}, u32[]{:S(2)}) %collective-permute-start.54) | collective-permute-done | bytes 1327136 | tf_op jit(solution)/shard_map/ppermute | solution.py:66
  576.2 8.1 shard_map.222
  584.3 17.6 %collective-permute-done.57.refs_4_ = bf16[3,288,384]{2,1,0:T(8,128)(2,1)} collective-permute-done((bf16[3,288,384]{2,1,0:T(8,128)(2,1)}, bf16[3,288,384]{2,1,0:T(8,128)(2,1)}, u32[]{:S(2)}, u32[]{:S(2)}) %collective-permute-start.57) | collective-permute-done | bytes 663584 | tf_op jit(solution)/shard_map/ppermute | solution.py:66
  601.8 17.0 %collective-permute-done.51.refs_6_ = bf16[3,288,768]{2,1,0:T(8,128)(2,1)} collective-permute-done((bf16[3,288,768]{2,1,0:T(8,128)(2,1)}, bf16[3,288,768]{2,1,0:T(8,128)(2,1)}, u32[]{:S(2)}, u32[]{:S(2)}) %collective-permute-start.51) | collective-permute-done | bytes 1327136 | tf_op jit(solution)/shard_map/ppermute | solution.py:66
  618.8 8.5 collective-permute-done.55.refs_0_
  632.9 8.7 shard_map.223
  641.6 6.0 collective-permute-done.59
  660.1 19.0 %shard_map.224 = (f32[33,288,256]{2,1,0:T(8,128)}, f32[33,288,256]{2,1,0:T(8,128)}, f32[33,3,128,128]{3,2,1,0:T(8,128)}) custom-call(s32[1]{0:T(128)} %bitcast.s_ref, bf16[3,288,768]{2,1,0:T(8,128)(2,1)} %collective-permute-done.55.refs_0_, bf16[3,288,768]{2,1,0:T(8,128)(2,1)} %get-tuple-element.289.refs_1_, ...), custom_call_target="tpu_custom_call" | custom-call | flops 3057647616 | bytes 31850496 | tf_op jit(solution)/shard_map/pallas_call | solution.py:825
  691.8 16.4 %collective-permute-done.71 = f32[6,128,128]{2,1,0:T(8,128)} collective-permute-done((f32[6,128,128]{2,1,0:T(8,128)S(1)}, f32[6,128,128]{2,1,0:T(8,128)}, u32[]{:S(2)}, u32[]{:S(2)}) %collective-permute-start.71) | collective-permute-done | bytes 393248 | tf_op jit(solution)/shard_map/ppermute | solution.py:66
  709.0 7.3 collective-permute-done.72
  728.3 5.5 collective-permute-done.73
  735.8 25.8 %collective-permute-done.74 = bf16[2,512,256]{2,1,0:T(8,128)(2,1)S(1)} collective-permute-done((bf16[2,512,256]{2,1,0:T(8,128)(2,1)S(1)}, bf16[2,512,256]{2,1,0:T(8,128)(2,1)S(1)}, u32[]{:S(2)}, u32[]{:S(2)}) %collective-permute-start.74) | collective-permute-done | bytes 524320 | tf_op jit(solution)/shard_map/ppermute | solution.py:66
  772.6 5.1 shard_map.225
  777.6 14.0 %collective-permute-done.79 = bf16[4,288,256]{2,1,0:T(8,128)(2,1)} collective-permute-done((bf16[4,288,256]{2,1,0:T(8,128)(2,1)}, bf16[4,288,256]{2,1,0:T(8,128)(2,1)}, u32[]{:S(2)}, u32[]{:S(2)}) %collective-permute-start.79) | collective-permute-done | bytes 589856 | tf_op jit(solution)/shard_map/ppermute | solution.py:66
  799.3 7.4 shard_map.226
  811.8 4.6 shard_map.227
  856.1 4.7 collective-permute-done.92
  890.9 4.8 collective-permute-done.96
  905.6 6.1 collective-permute-done.104
  964.8 6.2 shard_map.229.refs_3_
  974.1 6.1 shard_map.230.refs_3_
  985.9 6.1 shard_map.232
  (600 shorter events, 333.9 us)
Async XLA Ops:
  4.8 36.2 %collective-permute-start.6 = (bf16[4,288,256]{2,1,0:T(8,128)(2,1)}, bf16[4,288,256]{2,1,0:T(8,128)(2,1)}, u32[]{:S(2)}, u32[]{:S(2)}) collective-permute-start(bf16[4,288,256]{2,1,0:T(8,128)(2,1)} %slice.378), channel_id=1, source_target_pairs={{0,8},{8,16},{16,24},{24,28},{28,20},{20,12},{12,4},{4,0},{1,9},{9... | collective-permute-start | bytes 1769480 | tf_op jit(solution)/shard_map/ppermute | solution.py:79
  7.8 33.6 %collective-permute-start.7 = (bf16[4,288,256]{2,1,0:T(8,128)(2,1)}, bf16[4,288,256]{2,1,0:T(8,128)(2,1)}, u32[]{:S(2)}, u32[]{:S(2)}) collective-permute-start(bf16[4,288,256]{2,1,0:T(8,128)(2,1)} %slice.378), channel_id=1, source_target_pairs={{8,0},{16,8},{24,16},{28,24},{20,28},{12,20},{4,12},{0,4},{9,1},{1... | collective-permute-start | bytes 1769480 | tf_op jit(solution)/shard_map/ppermute | solution.py:79
  13.8 72.2 %collective-permute-start.2 = (bf16[3,288,768]{2,1,0:T(8,128)(2,1)}, bf16[3,288,768]{2,1,0:T(8,128)(2,1)}, u32[]{:S(2)}, u32[]{:S(2)}) collective-permute-start(bf16[3,288,768]{2,1,0:T(8,128)(2,1)} %get-tuple-element.201.refs_0_), channel_id=1, source_target_pairs={{0,8},{4,12},{8,0},{12,4},{16,24},{20,28},{24,16},{28,20},{1,9},{5... | collective-permute-start | bytes 3981320 | tf_op jit(solution)/shard_map/ppermute | solution.py:66
  15.8 70.2 %collective-permute-start.3 = (bf16[3,288,768]{2,1,0:T(8,128)(2,1)}, bf16[3,288,768]{2,1,0:T(8,128)(2,1)}, u32[]{:S(2)}, u32[]{:S(2)}) collective-permute-start(bf16[3,288,768]{2,1,0:T(8,128)(2,1)} %get-tuple-element.201.refs_0_), channel_id=1, source_target_pairs={{0,4},{4,0},{8,12},{12,8},{16,20},{20,16},{24,28},{28,24},{1,5},{5... | collective-permute-start | bytes 3981320 | tf_op jit(solution)/shard_map/ppermute | solution.py:66
  45.1 35.8 %collective-permute-start.5 = (bf16[256,2432]{1,0:T(8,128)(2,1)S(1)}, bf16[256,2432]{1,0:T(8,128)(2,1)S(1)}, u32[]{:S(2)}, u32[]{:S(2)}) collective-permute-start(bf16[256,2432]{1,0:T(8,128)(2,1)S(1)} %pad_maximum_fusion.4), channel_id=1, source_target_pairs={{0,1},{1,0},{2,3},{3,2},{4,5},{5,4},{6,7},{7,6},{8,9},{9,8},{10,11... | collective-permute-start | bytes 3735560 | tf_op jit(solution)/shard_map/ppermute | solution.py:79
  97.2 31.8 %collective-permute-start.18 = (bf16[1616,256]{1,0:T(8,128)(2,1)}, bf16[1616,256]{1,0:T(8,128)(2,1)}, u32[]{:S(2)}, u32[]{:S(2)}) collective-permute-start(bf16[1616,256]{1,0:T(8,128)(2,1)} %fusion.35), channel_id=1, source_target_pairs={{8,0},{16,8},{24,16},{28,24},{20,28},{12,20},{4,12},{0,4},{9,1},{1... | collective-permute-start | bytes 2482184 | tf_op jit(solution)/shard_map/ppermute | solution.py:79
  97.9 109.3 %collective-permute-start.16 = (bf16[3,288,384]{2,1,0:T(8,128)(2,1)}, bf16[3,288,384]{2,1,0:T(8,128)(2,1)}, u32[]{:S(2)}, u32[]{:S(2)}) collective-permute-start(bf16[3,288,384]{2,1,0:T(8,128)(2,1)} %get-tuple-element.200.refs_8_), channel_id=1, source_target_pairs={{0,8},{4,12},{8,0},{12,4},{16,24},{20,28},{24,16},{28,20},{1,9},{5... | collective-permute-start | bytes 1990664 | tf_op jit(solution)/shard_map/ppermute | solution.py:66
  101.0 106.2 %collective-permute-start.15 = (bf16[3,288,768]{2,1,0:T(8,128)(2,1)}, bf16[3,288,768]{2,1,0:T(8,128)(2,1)S(1)}, u32[]{:S(2)}, u32[]{:S(2)}) collective-permute-start(bf16[3,288,768]{2,1,0:T(8,128)(2,1)} %collective-permute-done.2.refs_2_), channel_id=1, source_target_pairs={{0,4},{4,0},{8,12},{12,8},{16,20},{20,16},{24,28},{28,24},{1,5},{5... | collective-permute-start | bytes 3981320 | tf_op jit(solution)/shard_map/ppermute | solution.py:66
  102.1 105.0 %collective-permute-start.14 = (bf16[128,2304]{1,0:T(8,128)(2,1)S(1)}, bf16[128,2304]{1,0:T(8,128)(2,1)S(1)}, u32[]{:S(2)}, u32[]{:S(2)}) collective-permute-start(bf16[128,2304]{1,0:T(8,128)(2,1)S(1)} %copy-done.9), channel_id=1, source_target_pairs={{0,16},{4,20},{8,24},{12,28},{16,0},{20,4},{24,8},{28,12},{1,17},{... | collective-permute-start | bytes 1769480 | tf_op jit(solution)/shard_map/ppermute | solution.py:66
  117.5 43.3 %collective-permute-start.19 = (bf16[1616,256]{1,0:T(8,128)(2,1)}, bf16[1616,256]{1,0:T(8,128)(2,1)S(1)}, u32[]{:S(2)}, u32[]{:S(2)}) collective-permute-start(bf16[1616,256]{1,0:T(8,128)(2,1)} %collective-permute-done.17), channel_id=1, source_target_pairs={{0,8},{8,16},{16,24},{24,28},{28,20},{20,12},{12,4},{4,0},{1,9},{9... | collective-permute-start | bytes 2482184 | tf_op jit(solution)/shard_map/ppermute | solution.py:79
  129.0 31.8 %collective-permute-start.20 = (bf16[1616,256]{1,0:T(8,128)(2,1)}, bf16[1616,256]{1,0:T(8,128)(2,1)S(1)}, u32[]{:S(2)}, u32[]{:S(2)}) collective-permute-start(bf16[1616,256]{1,0:T(8,128)(2,1)} %collective-permute-done.18), channel_id=1, source_target_pairs={{8,0},{16,8},{24,16},{28,24},{20,28},{12,20},{4,12},{0,4},{9,1},{1... | collective-permute-start | bytes 2482184 | tf_op jit(solution)/shard_map/ppermute | solution.py:79
  190.2 33.0 %collective-permute-start.1 = (bf16[3,288,384]{2,1,0:T(8,128)(2,1)}, bf16[3,288,384]{2,1,0:T(8,128)(2,1)}, u32[]{:S(2)}, u32[]{:S(2)}) collective-permute-start(bf16[3,288,384]{2,1,0:T(8,128)(2,1)} %get-tuple-element.200.refs_8_), channel_id=1, source_target_pairs={{0,4},{4,0},{8,12},{12,8},{16,20},{20,16},{24,28},{28,24},{1,5},{5... | collective-permute-start | bytes 1990664 | tf_op jit(solution)/shard_map/ppermute | solution.py:66
  192.0 53.5 %collective-permute-start = (bf16[3,288,768]{2,1,0:T(8,128)(2,1)}, bf16[3,288,768]{2,1,0:T(8,128)(2,1)}, u32[]{:S(2)}, u32[]{:S(2)}) collective-permute-start(bf16[3,288,768]{2,1,0:T(8,128)(2,1)} %get-tuple-element.199), channel_id=1, source_target_pairs={{0,16},{4,20},{8,24},{12,28},{16,0},{20,4},{24,8},{28,12},{1,17},{... | collective-permute-start | bytes 3981320 | tf_op jit(solution)/shard_map/ppermute | solution.py:66
  208.9 36.6 %collective-permute-start.26 = (bf16[256,2304]{1,0:T(8,128)(2,1)}, bf16[256,2304]{1,0:T(8,128)(2,1)}, u32[]{:S(2)}, u32[]{:S(2)}) collective-permute-start(bf16[256,2304]{1,0:T(8,128)(2,1)} %pad_maximum_fusion.5), channel_id=1, source_target_pairs={{0,2},{1,3},{2,0},{3,1},{4,6},{5,7},{6,4},{7,5},{8,10},{9,11},{10,... | collective-permute-start | bytes 3538952 | tf_op jit(solution)/shard_map/ppermute | solution.py:66
  210.7 34.7 %collective-permute-start.25 = (bf16[3,288,384]{2,1,0:T(8,128)(2,1)}, bf16[3,288,384]{2,1,0:T(8,128)(2,1)}, u32[]{:S(2)}, u32[]{:S(2)}) collective-permute-start(bf16[3,288,384]{2,1,0:T(8,128)(2,1)} %collective-permute-done.16.refs_10_), channel_id=1, source_target_pairs={{0,4},{4,0},{8,12},{12,8},{16,20},{20,16},{24,28},{28,24},{1,5},{5... | collective-permute-start | bytes 1990664 | tf_op jit(solution)/shard_map/ppermute | solution.py:66
  245.5 30.8 %collective-permute-start.31 = (bf16[3,288,384]{2,1,0:T(8,128)(2,1)}, bf16[3,288,384]{2,1,0:T(8,128)(2,1)S(1)}, u32[]{:S(2)}, u32[]{:S(2)}) collective-permute-start(bf16[3,288,384]{2,1,0:T(8,128)(2,1)} %get-tuple-element.220), channel_id=1, source_target_pairs={{0,16},{4,20},{8,24},{12,28},{16,0},{20,4},{24,8},{28,12},{1,17},{... | collective-permute-start | bytes 1990664 | tf_op jit(solution)/shard_map/ppermute | solution.py:66
  245.6 46.0 %collective-permute-start.29 = (bf16[3,288,768]{2,1,0:T(8,128)(2,1)}, bf16[3,288,768]{2,1,0:T(8,128)(2,1)S(1)}, u32[]{:S(2)}, u32[]{:S(2)}) collective-permute-start(bf16[3,288,768]{2,1,0:T(8,128)(2,1)} %collective-permute-done.refs_4_), channel_id=1, source_target_pairs={{0,8},{4,12},{8,0},{12,4},{16,24},{20,28},{24,16},{28,20},{1,9},{5... | collective-permute-start | bytes 3981320 | tf_op jit(solution)/shard_map/ppermute | solution.py:66
  246.9 44.7 %collective-permute-start.30 = (bf16[3,288,768]{2,1,0:T(8,128)(2,1)}, bf16[3,288,768]{2,1,0:T(8,128)(2,1)S(1)}, u32[]{:S(2)}, u32[]{:S(2)}) collective-permute-start(bf16[3,288,768]{2,1,0:T(8,128)(2,1)} %collective-permute-done.refs_4_), channel_id=1, source_target_pairs={{0,4},{4,0},{8,12},{12,8},{16,20},{20,16},{24,28},{28,24},{1,5},{5... | collective-permute-start | bytes 3981320 | tf_op jit(solution)/shard_map/ppermute | solution.py:66
  250.1 41.5 %collective-permute-start.28 = (bf16[128,2304]{1,0:T(8,128)(2,1)S(1)}, bf16[128,2304]{1,0:T(8,128)(2,1)S(1)}, u32[]{:S(2)}, u32[]{:S(2)}) collective-permute-start(bf16[128,2304]{1,0:T(8,128)(2,1)S(1)} %slice.465), channel_id=1, source_target_pairs={{0,2},{1,3},{2,0},{3,1},{4,6},{5,7},{6,4},{7,5},{8,10},{9,11},{10,... | collective-permute-start | bytes 1769480 | tf_op jit(solution)/shard_map/ppermute | solution.py:66
  291.6 30.8 %collective-permute-start.34 = (bf16[3,288,384]{2,1,0:T(8,128)(2,1)S(1)}, bf16[3,288,384]{2,1,0:T(8,128)(2,1)S(1)}, u32[]{:S(2)}, u32[]{:S(2)}) collective-permute-start(bf16[3,288,384]{2,1,0:T(8,128)(2,1)S(1)} %collective-permute-done.31.refs_12_), channel_id=1, source_target_pairs={{0,8},{4,12},{8,0},{12,4},{16,24},{20,28},{24,16},{28,20},{1,9},{5... | collective-permute-start | bytes 1990664 | tf_op jit(solution)/shard_map/ppermute | solution.py:66
  291.8 30.5 %collective-permute-start.35 = (bf16[3,288,384]{2,1,0:T(8,128)(2,1)S(1)}, bf16[3,288,384]{2,1,0:T(8,128)(2,1)S(1)}, u32[]{:S(2)}, u32[]{:S(2)}) collective-permute-start(bf16[3,288,384]{2,1,0:T(8,128)(2,1)S(1)} %collective-permute-done.31.refs_12_), channel_id=1, source_target_pairs={{0,4},{4,0},{8,12},{12,8},{16,20},{20,16},{24,28},{28,24},{1,5},{5... | collective-permute-start | bytes 1990664 | tf_op jit(solution)/shard_map/ppermute | solution.py:66
  292.2 44.5 %collective-permute-start.33 = (bf16[3,288,768]{2,1,0:T(8,128)(2,1)S(1)}, bf16[3,288,768]{2,1,0:T(8,128)(2,1)S(1)}, u32[]{:S(2)}, u32[]{:S(2)}) collective-permute-start(bf16[3,288,768]{2,1,0:T(8,128)(2,1)S(1)} %collective-permute-done.29.refs_6_), channel_id=1, source_target_pairs={{0,4},{4,0},{8,12},{12,8},{16,20},{20,16},{24,28},{28,24},{1,5},{5... | collective-permute-start | bytes 3981320 | tf_op jit(solution)/shard_map/ppermute | solution.py:66
  294.5 27.9 %collective-permute-start.32 = (bf16[128,2304]{1,0:T(8,128)(2,1)S(1)}, bf16[128,2304]{1,0:T(8,128)(2,1)S(1)}, u32[]{:S(2)}, u32[]{:S(2)}) collective-permute-start(bf16[128,2304]{1,0:T(8,128)(2,1)S(1)} %multiply_convert_fusion), channel_id=1, source_target_pairs={{0,16},{4,20},{8,24},{12,28},{16,0},{20,4},{24,8},{28,12},{1,17},{... | collective-permute-start | bytes 1769480 | tf_op jit(solution)/shard_map/ppermute | solution.py:66
  336.7 28.6 %collective-permute-start.38 = (bf16[512,2304]{1,0:T(8,128)(2,1)S(1)}, bf16[512,2304]{1,0:T(8,128)(2,1)}, u32[]{:S(2)}, u32[]{:S(2)}) collective-permute-start(bf16[512,2304]{1,0:T(8,128)(2,1)S(1)} %constant_dynamic-update-slice_fusion.y0), channel_id=1, source_target_pairs={{0,1},{1,0},{2,3},{3,2},{4,5},{5,4},{6,7},{7,6},{8,9},{9,8},{10,11... | collective-permute-start | bytes 7077896 | tf_op jit(solution)/shard_map/ppermute | solution.py:66
  336.8 28.4 %collective-permute-start.36 = (bf16[256,2304]{1,0:T(8,128)(2,1)S(1)}, bf16[256,2304]{1,0:T(8,128)(2,1)S(1)}, u32[]{:S(2)}, u32[]{:S(2)}) collective-permute-start(bf16[256,2304]{1,0:T(8,128)(2,1)S(1)} %pad_maximum_fusion.6), channel_id=1, source_target_pairs={{0,2},{1,3},{2,0},{3,1},{4,6},{5,7},{6,4},{7,5},{8,10},{9,11},{10,... | collective-permute-start | bytes 3538952 | tf_op jit(solution)/shard_map/ppermute | solution.py:66
  422.4 31.5 %collective-permute-start.40 = (bf16[3,288,768]{2,1,0:T(8,128)(2,1)}, bf16[3,288,768]{2,1,0:T(8,128)(2,1)}, u32[]{:S(2)}, u32[]{:S(2)}) collective-permute-start(bf16[3,288,768]{2,1,0:T(8,128)(2,1)} %get-tuple-element.239), channel_id=1, source_target_pairs={{0,4},{4,0},{8,12},{12,8},{16,20},{20,16},{24,28},{28,24},{1,5},{5... | collective-permute-start | bytes 3981320 | tf_op jit(solution)/shard_map/ppermute | solution.py:66
  453.9 46.3 %collective-permute-start.44 = (bf16[3,288,768]{2,1,0:T(8,128)(2,1)}, bf16[3,288,768]{2,1,0:T(8,128)(2,1)S(1)}, u32[]{:S(2)}, u32[]{:S(2)}) collective-permute-start(bf16[3,288,768]{2,1,0:T(8,128)(2,1)} %get-tuple-element.251), channel_id=1, source_target_pairs={{0,4},{4,0},{8,12},{12,8},{16,20},{20,16},{24,28},{28,24},{1,5},{5... | collective-permute-start | bytes 3981320 | tf_op jit(solution)/shard_map/ppermute | solution.py:66
  456.2 45.7 %collective-permute-start.43 = (bf16[3,288,768]{2,1,0:T(8,128)(2,1)S(1)}, bf16[3,288,768]{2,1,0:T(8,128)(2,1)S(1)}, u32[]{:S(2)}, u32[]{:S(2)}) collective-permute-start(bf16[3,288,768]{2,1,0:T(8,128)(2,1)S(1)} %add_convert_fusion.2), channel_id=1, source_target_pairs={{0,8},{4,12},{8,0},{12,4},{16,24},{20,28},{24,16},{28,20},{1,9},{5... | collective-permute-start | bytes 3981320 | tf_op jit(solution)/shard_map/ppermute | solution.py:66
  459.3 42.6 %collective-permute-start.42 = (bf16[256,2304]{1,0:T(8,128)(2,1)S(1)}, bf16[256,2304]{1,0:T(8,128)(2,1)S(1)}, u32[]{:S(2)}, u32[]{:S(2)}) collective-permute-start(bf16[256,2304]{1,0:T(8,128)(2,1)S(1)} %slice.462), channel_id=1, source_target_pairs={{0,2},{1,3},{2,0},{3,1},{4,6},{5,7},{6,4},{7,5},{8,10},{9,11},{10,... | collective-permute-start | bytes 3538952 | tf_op jit(solution)/shard_map/ppermute | solution.py:66
  460.9 39.0 %collective-permute-start.45 = (bf16[3,288,384]{2,1,0:T(8,128)(2,1)S(1)}, bf16[3,288,384]{2,1,0:T(8,128)(2,1)S(1)}, u32[]{:S(2)}, u32[]{:S(2)}) collective-permute-start(bf16[3,288,384]{2,1,0:T(8,128)(2,1)S(1)} %copy-done.76), channel_id=1, source_target_pairs={{0,4},{4,0},{8,12},{12,8},{16,20},{20,16},{24,28},{28,24},{1,5},{5... | collective-permute-start | bytes 1990664 | tf_op jit(solution)/shard_map/ppermute | solution.py:66
  461.9 70.0 %collective-permute-start.50 = (bf16[512,2304]{1,0:T(8,128)(2,1)S(1)}, bf16[512,2304]{1,0:T(8,128)(2,1)S(1)}, u32[]{:S(2)}, u32[]{:S(2)}) collective-permute-start(bf16[512,2304]{1,0:T(8,128)(2,1)S(1)} %copy-done.65), channel_id=1, source_target_pairs={{0,1},{1,0},{2,3},{3,2},{4,5},{5,4},{6,7},{7,6},{8,9},{9,8},{10,11... | collective-permute-start | bytes 7077896 | tf_op jit(solution)/shard_map/ppermute | solution.py:66
  500.2 31.7 %collective-permute-start.48 = (bf16[3,288,384]{2,1,0:T(8,128)(2,1)S(1)}, bf16[3,288,384]{2,1,0:T(8,128)(2,1)S(1)}, u32[]{:S(2)}, u32[]{:S(2)}) collective-permute-start(bf16[3,288,384]{2,1,0:T(8,128)(2,1)S(1)} %copy-done.72), channel_id=1, source_target_pairs={{0,4},{4,0},{8,12},{12,8},{16,20},{20,16},{24,28},{28,24},{1,5},{5... | collective-permute-start | bytes 1990664 | tf_op jit(solution)/shard_map/ppermute | solution.py:66
  502.1 29.8 %collective-permute-start.49 = (bf16[3,288,384]{2,1,0:T(8,128)(2,1)S(1)}, bf16[3,288,384]{2,1,0:T(8,128)(2,1)S(1)}, u32[]{:S(2)}, u32[]{:S(2)}) collective-permute-start(bf16[3,288,384]{2,1,0:T(8,128)(2,1)S(1)} %add_convert_fusion.5), channel_id=1, source_target_pairs={{0,8},{4,12},{8,0},{12,4},{16,24},{20,28},{24,16},{28,20},{1,9},{5... | collective-permute-start | bytes 1990664 | tf_op jit(solution)/shard_map/ppermute | solution.py:66
  517.7 42.7 %collective-permute-start.54 = (bf16[3,288,768]{2,1,0:T(8,128)(2,1)S(1)}, bf16[3,288,768]{2,1,0:T(8,128)(2,1)S(1)}, u32[]{:S(2)}, u32[]{:S(2)}) collective-permute-start(bf16[3,288,768]{2,1,0:T(8,128)(2,1)S(1)} %copy-done.67), channel_id=1, source_target_pairs={{0,4},{4,0},{8,12},{12,8},{16,20},{20,16},{24,28},{28,24},{1,5},{5... | collective-permute-start | bytes 3981320 | tf_op jit(solution)/shard_map/ppermute | solution.py:66
  532.2 30.1 %collective-permute-start.53 = (bf16[3,288,384]{2,1,0:T(8,128)(2,1)S(1)}, bf16[3,288,384]{2,1,0:T(8,128)(2,1)S(1)}, u32[]{:S(2)}, u32[]{:S(2)}) collective-permute-start(bf16[3,288,384]{2,1,0:T(8,128)(2,1)S(1)} %add_convert_fusion.4), channel_id=1, source_target_pairs={{0,16},{4,20},{8,24},{12,28},{16,0},{20,4},{24,8},{28,12},{1,17},{... | collective-permute-start | bytes 1990664 | tf_op jit(solution)/shard_map/ppermute | solution.py:66
  539.1 62.8 %collective-permute-start.56 = (bf16[3,288,768]{2,1,0:T(8,128)(2,1)}, bf16[3,288,768]{2,1,0:T(8,128)(2,1)}, u32[]{:S(2)}, u32[]{:S(2)}) collective-permute-start(bf16[3,288,768]{2,1,0:T(8,128)(2,1)} %get-tuple-element.270), channel_id=1, source_target_pairs={{0,4},{4,0},{8,12},{12,8},{16,20},{20,16},{24,28},{28,24},{1,5},{5... | collective-permute-start | bytes 3981320 | tf_op jit(solution)/shard_map/ppermute | solution.py:66
  539.4 62.5 %collective-permute-start.57 = (bf16[3,288,384]{2,1,0:T(8,128)(2,1)}, bf16[3,288,384]{2,1,0:T(8,128)(2,1)}, u32[]{:S(2)}, u32[]{:S(2)}) collective-permute-start(bf16[3,288,384]{2,1,0:T(8,128)(2,1)} %get-tuple-element.271), channel_id=1, source_target_pairs={{0,4},{4,0},{8,12},{12,8},{16,20},{20,16},{24,28},{28,24},{1,5},{5... | collective-permute-start | bytes 1990664 | tf_op jit(solution)/shard_map/ppermute | solution.py:66
  560.3 58.5 %collective-permute-start.51 = (bf16[3,288,768]{2,1,0:T(8,128)(2,1)}, bf16[3,288,768]{2,1,0:T(8,128)(2,1)}, u32[]{:S(2)}, u32[]{:S(2)}) collective-permute-start(bf16[3,288,768]{2,1,0:T(8,128)(2,1)} %add_convert_fusion.1), channel_id=1, source_target_pairs={{0,16},{4,20},{8,24},{12,28},{16,0},{20,4},{24,8},{28,12},{1,17},{... | collective-permute-start | bytes 3981320 | tf_op jit(solution)/shard_map/ppermute | solution.py:66
  568.0 59.3 %collective-permute-start.55 = (bf16[3,288,768]{2,1,0:T(8,128)(2,1)}, bf16[3,288,768]{2,1,0:T(8,128)(2,1)}, u32[]{:S(2)}, u32[]{:S(2)}) collective-permute-start(bf16[3,288,768]{2,1,0:T(8,128)(2,1)} %add_convert_fusion), channel_id=1, source_target_pairs={{0,8},{4,12},{8,0},{12,4},{16,24},{20,28},{24,16},{28,20},{1,9},{5... | collective-permute-start | bytes 3981320 | tf_op jit(solution)/shard_map/ppermute | solution.py:66
  631.4 47.7 %collective-permute-start.66 = (bf16[256,2304]{1,0:T(8,128)(2,1)}, bf16[256,2304]{1,0:T(8,128)(2,1)S(1)}, u32[]{:S(2)}, u32[]{:S(2)}) collective-permute-start(bf16[256,2304]{1,0:T(8,128)(2,1)} %slice.461), channel_id=1, source_target_pairs={{0,2},{1,3},{2,0},{3,1},{4,6},{5,7},{6,4},{7,5},{8,10},{9,11},{10,... | collective-permute-start | bytes 3538952 | tf_op jit(solution)/shard_map/ppermute | solution.py:66
  682.0 34.3 %collective-permute-start.70 = (bf16[4,288,256]{2,1,0:T(8,128)(2,1)S(1)}, bf16[4,288,256]{2,1,0:T(8,128)(2,1)}, u32[]{:S(2)}, u32[]{:S(2)}) collective-permute-start(bf16[4,288,256]{2,1,0:T(8,128)(2,1)S(1)} %pad_maximum_fusion.14), channel_id=1, source_target_pairs={{8,0},{16,8},{24,16},{28,24},{20,28},{12,20},{4,12},{0,4},{9,1},{1... | collective-permute-start | bytes 1769480 | tf_op jit(solution)/shard_map/ppermute | solution.py:66
  683.2 33.9 %collective-permute-start.69 = (bf16[4,288,256]{2,1,0:T(8,128)(2,1)}, bf16[4,288,256]{2,1,0:T(8,128)(2,1)}, u32[]{:S(2)}, u32[]{:S(2)}) collective-permute-start(bf16[4,288,256]{2,1,0:T(8,128)(2,1)} %pad_maximum_fusion.13), channel_id=1, source_target_pairs={{0,8},{8,16},{16,24},{24,28},{28,20},{20,12},{12,4},{4,0},{1,9},{9... | collective-permute-start | bytes 1769480 | tf_op jit(solution)/shard_map/ppermute | solution.py:66
  722.4 39.2 %collective-permute-start.78 = (f32[12,128,128]{2,1,0:T(8,128)S(1)}, f32[12,128,128]{2,1,0:T(8,128)S(1)}, u32[]{:S(2)}, u32[]{:S(2)}) collective-permute-start(f32[12,128,128]{2,1,0:T(8,128)S(1)} %pad_maximum_fusion.11), channel_id=1, source_target_pairs={{8,0},{16,8},{24,16},{28,24},{20,28},{12,20},{4,12},{0,4},{9,1},{1... | collective-permute-start | bytes 2359304 | tf_op jit(solution)/shard_map/ppermute | solution.py:66
  722.9 38.8 %collective-permute-start.77 = (f32[12,128,128]{2,1,0:T(8,128)S(1)}, f32[12,128,128]{2,1,0:T(8,128)S(1)}, u32[]{:S(2)}, u32[]{:S(2)}) collective-permute-start(f32[12,128,128]{2,1,0:T(8,128)S(1)} %pad_maximum_fusion.10), channel_id=1, source_target_pairs={{0,8},{8,16},{16,24},{24,28},{28,20},{20,12},{12,4},{4,0},{1,9},{9... | collective-permute-start | bytes 2359304 | tf_op jit(solution)/shard_map/ppermute | solution.py:66
  726.2 35.4 %collective-permute-start.75 = (bf16[4,288,256]{2,1,0:T(8,128)(2,1)S(1)}, bf16[4,288,256]{2,1,0:T(8,128)(2,1)S(1)}, u32[]{:S(2)}, u32[]{:S(2)}) collective-permute-start(bf16[4,288,256]{2,1,0:T(8,128)(2,1)S(1)} %get-tuple-element.420), channel_id=1, source_target_pairs={{0,8},{8,16},{16,24},{24,28},{28,20},{20,12},{12,4},{4,0},{1,9},{9... | collective-permute-start | bytes 1769480 | tf_op jit(solution)/shard_map/ppermute | solution.py:66
  726.5 35.1 %collective-permute-start.76 = (bf16[4,288,256]{2,1,0:T(8,128)(2,1)S(1)}, bf16[4,288,256]{2,1,0:T(8,128)(2,1)S(1)}, u32[]{:S(2)}, u32[]{:S(2)}) collective-permute-start(bf16[4,288,256]{2,1,0:T(8,128)(2,1)S(1)} %get-tuple-element.419), channel_id=1, source_target_pairs={{8,0},{16,8},{24,16},{28,24},{20,28},{12,20},{4,12},{0,4},{9,1},{1... | collective-permute-start | bytes 1769480 | tf_op jit(solution)/shard_map/ppermute | solution.py:66
  764.4 28.5 %collective-permute-start.81 = (f32[12,128,128]{2,1,0:T(8,128)}, f32[12,128,128]{2,1,0:T(8,128)}, u32[]{:S(2)}, u32[]{:S(2)}) collective-permute-start(f32[12,128,128]{2,1,0:T(8,128)} %get-tuple-element.410), channel_id=1, source_target_pairs={{0,8},{8,16},{16,24},{24,28},{28,20},{20,12},{12,4},{4,0},{1,9},{9... | collective-permute-start | bytes 2359304 | tf_op jit(solution)/shard_map/ppermute | solution.py:66
  919.3 28.8 %collective-permute-start.113 = (bf16[64,2304]{1,0:T(8,128)(2,1)}, bf16[64,2304]{1,0:T(8,128)(2,1)}, u32[]{:S(2)}, u32[]{:S(2)}) collective-permute-start(bf16[64,2304]{1,0:T(8,128)(2,1)} %get-tuple-element.449), channel_id=1, source_target_pairs={{0,16},{4,20},{8,24},{12,28},{16,0},{20,4},{24,8},{28,12},{1,17},{... | collective-permute-start | bytes 884744 | tf_op jit(solution)/shard_map/ppermute | solution.py:66
  (158 other events, 2367.5 us)
